TPU v7x, 256 devices: a whole 4x4x8 slice. The times are simulated.
256 devices in a mesh: tile: 8 (over z), grp: 32 (over x, y, core).
Axes of the slice: x: 4, y: 4, z: 8, core: 2. Of those that a mesh axis runs over, the one named last changes fastest.
Arguments:
- inputs: bfloat16 [2, 64, 64, 2112], P(None, 'tile', None, 'grp'), may hold values from -6 to 6
- cotangent: bfloat16 [2, 64, 64, 2112], P(None, 'tile', None, 'grp'), may hold values from -6 to 6
- first_weight: bfloat16 [2112, 2112], P(None, 'grp'), may hold values from -0.25 to 0.25
- first_bias: float32 [2112], P('grp'), may hold values from -3 to 3
- conv_weight: bfloat16 [2112, 9, 264], P('grp'), may hold values from -0.125 to 0.125
- conv_bias: float32 [2112], P('grp'), may hold values from -3 to 3
- squeeze_weight: bfloat16 [2112, 528], P('grp'), may hold values from -0.125 to 0.125
- squeeze_bias: float32 [528], replicated, may hold values from -3 to 3
- excite_weight: bfloat16 [528, 2112], P(None, 'grp'), may hold values from -0.25 to 0.25
- excite_bias: float32 [2112], P('grp'), may hold values from -0.5 to 0.5
- second_weight: bfloat16 [2112, 2112], P('grp'), may hold values from -0.25 to 0.25
- first_basis: float32 [2112, 256], replicated, may hold values from -0.125 to 0.125
- second_basis: float32 [2112, 256], P('grp'), may hold values from -0.125 to 0.125
Outputs:
- block_out: bfloat16 [2, 64, 64, 2112], P(None, 'tile', None, 'grp')
- input_grad: bfloat16 [2, 64, 64, 2112], P(None, 'tile', None, 'grp')
- first_grad: float32 [2112, 2112], P(None, 'grp')
- second_grad: float32 [2112, 2112], P('grp')
- conv_grad: float32 [2112, 9, 264], P('grp')
- squeeze_grad: float32 [2112, 528], P('grp')
- excite_grad: float32 [528, 2112], P(None, 'grp')
All inputs are finite; a program needn't handle non-finite values.
Results may differ from a plain program's by a relative error of at most 0.015.
Values may be sent and summed in bfloat16 or wider, within the bound.
A program may use at most 128 MiB of HBM per device.

v0:
```python
import math

import jax
import jax.numpy as jnp
from jax import lax
from jax.sharding import PartitionSpec as P

highest = lax.Precision.HIGHEST


def swapped(shard, axis, apart):
    return lax.ppermute(shard, axis, [(i, i ^ 1 << apart) for i in range(lax.axis_size(axis))])


def padded(shard, sides, width):
    for axis, dim in sides:
        size, length = (lax.axis_size(axis), shard.shape[dim])
        up = [(i, (i + 1) % size) for i in range(size - 1)]
        down = [(j, i) for i, j in up]
        last = lax.slice_in_dim(shard, length - width, length, axis=dim)
        leading = lax.slice_in_dim(shard, 0, width, axis=dim)
        before = lax.ppermute(last, axis, up)
        after = lax.ppermute(leading, axis, down)
        shard = jnp.concatenate([before, shard, after], axis=dim)
    return shard


def slope(value):
    sig = jax.nn.sigmoid(value)
    return sig * (1.0 + value * (1.0 - sig))


def tap_stack(framed, rows_dev, col_count, flipped):
    windows = []
    for tap_index in range(9):
        row_shift, col_shift = (tap_index // 3, tap_index % 3)
        if flipped:
            row_shift, col_shift = (2 - row_shift, 2 - col_shift)
        windows.append(
            framed[:, row_shift : row_shift + rows_dev, col_shift : col_shift + col_count]
        )
    return jnp.stack(windows, axis=3)


def per_device(
    inputs,
    cotangent,
    first_weight,
    first_bias,
    conv_weight,
    conv_bias,
    squeeze_weight,
    squeeze_bias,
    excite_weight,
    excite_bias,
    second_weight,
    first_basis,
    second_basis,
):
    images, rows_dev, col_count, ch_dev = inputs.shape
    channels = first_weight.shape[0]
    group_width = conv_weight.shape[2]
    pixels = images * rows_dev * col_count
    cell_area = rows_dev * lax.axis_size("tile") * col_count
    grad_scale = 1.0 / math.sqrt(images * cell_area)
    splits = group_width // ch_dev
    bit_count = splits.bit_length() - 1
    position = lax.axis_index("grp")
    everything = lax.all_gather(inputs, "grp", axis=3, tiled=True)
    flat_all = everything.reshape(pixels, channels)
    first_pre = jnp.dot(flat_all, first_weight, preferred_element_type=jnp.float32) + first_bias
    active = jax.nn.silu(first_pre).astype(jnp.bfloat16)
    group_feat = active.reshape(images, rows_dev, col_count, ch_dev)
    for bit_number in range(bit_count):
        partner = swapped(group_feat, "grp", bit_number)
        is_lower = position >> bit_number & 1 == 0
        group_feat = jnp.where(
            is_lower,
            jnp.concatenate([group_feat, partner], 3),
            jnp.concatenate([partner, group_feat], 3),
        )
    framed = padded(group_feat, (("tile", 1),), 1)
    framed = jnp.pad(framed, ((0, 0), (0, 0), (1, 1), (0, 0)))
    columns = tap_stack(framed, rows_dev, col_count, False).reshape(pixels, 9 * group_width)
    conv_pre = jnp.dot(
        columns, conv_weight.reshape(ch_dev, 9 * group_width).T, preferred_element_type=jnp.float32
    )
    conv_out = (conv_pre + conv_bias).reshape(images, rows_dev * col_count, ch_dev)
    hidden = jax.nn.silu(conv_out)
    local_sums = jnp.sum(hidden, axis=1)
    squeeze_matrix = squeeze_weight.astype(jnp.float32)
    means = lax.psum(local_sums, "tile") / cell_area
    squeeze_sum = lax.psum(jnp.dot(means, squeeze_matrix, precision=highest), "grp")
    squeeze_pre = squeeze_sum + squeeze_bias
    squeeze = jax.nn.silu(squeeze_pre)
    excite_matrix = excite_weight.astype(jnp.float32)
    excite = jax.nn.sigmoid(jnp.dot(squeeze, excite_matrix, precision=highest) + excite_bias)
    scaled = (hidden * excite[:, None, :]).astype(jnp.bfloat16).reshape(pixels, ch_dev)
    part = second_weight
    second = (
        lax.psum_scatter(
            lax.dot_general(
                part, scaled, (((0,), (1,)), ((), ())), preferred_element_type=jnp.float32
            ).astype(jnp.bfloat16),
            "grp",
            scatter_dimension=0,
            tiled=True,
        )
        .astype(jnp.float32)
        .T
    )
    total = inputs.reshape(pixels, ch_dev).astype(jnp.float32) + second
    block_out = jax.nn.silu(total).astype(jnp.bfloat16).reshape(images, rows_dev, col_count, ch_dev)
    back = (cotangent.reshape(pixels, ch_dev).astype(jnp.float32) * slope(total)).astype(
        jnp.bfloat16
    )
    back_all = lax.all_gather(
        back.reshape(images, rows_dev, col_count, ch_dev), "grp", axis=3, tiled=True
    ).reshape(pixels, channels)
    second_raw = jnp.dot(scaled.T, back_all, preferred_element_type=jnp.float32)
    scaled_back = jnp.dot(back_all, second_weight.T, preferred_element_type=jnp.float32).reshape(
        images, rows_dev * col_count, ch_dev
    )
    excite_part = jnp.sum(scaled_back * hidden, axis=1)
    excite_back = lax.psum(excite_part, "tile")
    sig_back = excite_back * excite * (1.0 - excite)
    excite_grad = jnp.dot(squeeze.T, sig_back, precision=highest) * grad_scale
    squeeze_part = jnp.dot(sig_back, excite_matrix.T, precision=highest)
    squeeze_back = lax.psum(squeeze_part, "grp") * slope(squeeze_pre)
    squeeze_grad = jnp.dot(means.T, squeeze_back, precision=highest) * grad_scale
    means_back = jnp.dot(squeeze_back, squeeze_matrix.T, precision=highest)
    hidden_back = (
        (scaled_back * excite[:, None, :] + means_back[:, None, :] / cell_area) * slope(conv_out)
    ).astype(jnp.bfloat16)
    hidden_flat = hidden_back.reshape(pixels, ch_dev)
    conv_part = jnp.dot(hidden_flat.T, columns, preferred_element_type=jnp.float32)
    back_frame = padded(hidden_back.reshape(images, rows_dev, col_count, ch_dev), (("tile", 1),), 1)
    back_frame = jnp.pad(back_frame, ((0, 0), (0, 0), (1, 1), (0, 0)))
    back_columns = tap_stack(back_frame, rows_dev, col_count, True).reshape(pixels, 9 * ch_dev)
    taps_first = conv_weight.transpose(1, 0, 2).reshape(9 * ch_dev, group_width)
    reduced = jnp.dot(back_columns, taps_first, preferred_element_type=jnp.float32)
    for bit_number in reversed(range(bit_count)):
        halves = reduced.reshape(pixels, 2, reduced.shape[1] // 2)
        own_bit = position >> bit_number & 1
        keeping = jnp.where(own_bit == 0, halves[:, 0], halves[:, 1])
        sending = jnp.where(own_bit == 0, halves[:, 1], halves[:, 0])
        reduced = keeping + swapped(sending, "grp", bit_number)
    active_grad = (reduced * slope(first_pre)).astype(jnp.bfloat16)
    first_raw = jnp.dot(flat_all.T, active_grad, preferred_element_type=jnp.float32)
    second_sum, conv_sum, first_sum = lax.psum((second_raw, conv_part, first_raw), "tile")
    first_grad = (
        jnp.dot(
            first_basis, jnp.dot(first_basis.T, first_sum, precision=highest), precision=highest
        )
        * grad_scale
    )
    coordinates = lax.psum(jnp.dot(second_basis.T, second_sum, precision=highest), "grp")
    second_grad = jnp.dot(second_basis, coordinates, precision=highest) * grad_scale
    conv_grad = conv_sum.reshape(ch_dev, 9, group_width) * grad_scale
    part = first_weight
    input_sum = (
        lax.psum_scatter(
            lax.dot_general(
                part, active_grad, (((1,), (1,)), ((), ())), preferred_element_type=jnp.float32
            ).astype(jnp.bfloat16),
            "grp",
            scatter_dimension=0,
            tiled=True,
        )
        .astype(jnp.float32)
        .T
    )
    input_grad = (
        (back.astype(jnp.float32) + input_sum)
        .astype(jnp.bfloat16)
        .reshape(images, rows_dev, col_count, ch_dev)
    )
    return (block_out, input_grad, first_grad, second_grad, conv_grad, squeeze_grad, excite_grad)


def solution(mesh):
    placed = (
        P(None, "tile", None, "grp"),
        P(None, "tile", None, "grp"),
        P(None, "grp"),
        P("grp"),
        P("grp", None, None),
        P("grp"),
        P("grp", None),
        P(),
        P(None, "grp"),
        P("grp"),
        P("grp", None),
        P(),
        P("grp", None),
    )
    return jax.shard_map(
        per_device,
        mesh=mesh,
        in_specs=placed,
        out_specs=(
            P(None, "tile", None, "grp"),
            P(None, "tile", None, "grp"),
            P(None, "grp"),
            P("grp", None),
            P("grp", None, None),
            P("grp", None),
            P(None, "grp"),
        ),
        check_vma=False,
    )
```

profile of v0, /device:TPU:2, one launch (start us, length us, event | category | flops | bytes accessed | tf_op | source)
XLA Modules:
  0.0 771.1 jit_solution(1695466168428520417)
XLA Ops:
  7.2 2.1 copy.115
  9.4 63.4 %all-gather.3.cloned.1.call-done = bf16[2,8,64,2112]{2,1,0,3:T(8,128)(2,1)} async-done(((bf16[2,8,64,66]{2,1,0,3:T(8,128)(2,1)}), bf16[2,8,64,2112]{2,1,0,3:T(8,128)(2,1)}) %all-gather.3.cloned.1.call-update) | async-done | bytes 4325392 | tf_op jit(solution)/shard_map/all_gather | solution.py:69
  72.7 11.3 %copy.116 = bf16[2,8,64,2112]{3,2,1,0:T(8,128)(2,1)} copy(bf16[2,8,64,2112]{2,1,0,3:T(8,128)(2,1)} %all-gather.3.cloned.1.call-done) | data formatting | bytes 8650752 | tf_op jit(solution)/shard_map/all_gather | solution.py:69
  84.1 4.5 multiply_convert_fusion.4
  92.2 14.2 %collective-permute-done.1 = bf16[2,8,64,132]{3,2,1,0:T(8,128)(2,1)S(1)} collective-permute-done((bf16[2,8,64,132]{3,2,1,0:T(8,128)(2,1)}, bf16[2,8,64,132]{3,2,1,0:T(8,128)(2,1)S(1)}, u32[]{:S(2)}, u32[]{:S(2)}) %collective-permute-start.1) | collective-permute-done | bytes 270368 | tf_op jit(solution)/shard_map/ppermute | solution.py:12
  107.6 2.0 maximum_select_fusion
  110.8 4.2 collective-permute-start.2
  118.5 2.0 copy.121
  120.5 2.4 reshape.165
  124.6 3.5 fusion.11
  129.3 2.6 fusion.24
  142.2 13.6 %reshape.164 = bf16[1024,2376]{0,1:T(8,128)(2,1)} reshape(bf16[2,8,64,9,264]{2,1,0,4,3:T(8,128)(2,1)} %fusion.16) | data formatting | bytes 9732096 | tf_op jit(solution)/shard_map/reshape | solution.py:84
  155.9 3.4 convolution_add_fusion.1
  159.8 17.3 %psum.56 = f32[2,66]{1,0:T(2,128)S(1)} all-reduce(f32[2,66]{1,0:T(2,128)S(1)} %fusion.49), channel_id=1, replica_groups=mesh['tile'=8,'grp'=32] {'tile'}, use_global_device_ids=true, to_apply=%region_1.2 | all-reduce | flops 132 | bytes 1056 | tf_op jit(solution)/shard_map/psum | solution.py:92
  177.2 54.0 %psum.57 = f32[2,528]{1,0:T(2,128)S(1)} all-reduce(f32[2,528]{1,0:T(2,128)S(1)} %fusion.51), channel_id=1, replica_groups=mesh['tile'=8,'grp'=32] {'grp'}, use_global_device_ids=true, to_apply=%region_2.3 | all-reduce | flops 1056 | bytes 8448 | tf_op jit(solution)/shard_map/psum | solution.py:93
  232.0 4.4 fusion.2
  236.4 68.5 %fusion = bf16[72,1024]{1,0:T(8,128)(2,1)S(1)} fusion(bf16[2112,1024]{1,0:T(8,128)(2,1)} %fusion.2), kind=kCustom, calls=%all-reduce-scatter | all-reduce-scatter fusion | flops 2359297 | bytes 4473856
  305.5 1.9 collective-permute-start.8
  307.4 1.9 collective-permute-start.9
  309.4 2.1 collective-permute-start.10
  316.7 4.5 collective-permute-done.10
  321.2 5.3 concatenate.74
  326.4 1.8 multiply_convert_fusion.1
  329.2 67.4 %all-gather.5.cloned.1.call-done = bf16[2,8,64,2112]{2,1,0,3:T(8,128)(2,1)} async-done(((bf16[2,8,64,66]{2,1,0,3:T(8,128)(2,1)}), bf16[2,8,64,2112]{2,1,0,3:T(8,128)(2,1)}) %all-gather.5.cloned.1.call-update) | async-done | bytes 4325392 | tf_op jit(solution)/shard_map/all_gather | solution.py:117
  396.6 11.3 %copy.126 = bf16[2,8,64,2112]{3,2,1,0:T(8,128)(2,1)} copy(bf16[2,8,64,2112]{2,1,0,3:T(8,128)(2,1)} %all-gather.5.cloned.1.call-done) | data formatting | bytes 8650752 | tf_op jit(solution)/shard_map/all_gather | solution.py:117
  408.0 4.0 multiply_reduce_fusion
  412.0 17.5 %psum.58 = f32[2,66]{1,0:T(2,128)S(1)} all-reduce(f32[2,66]{1,0:T(2,128)S(1)} %get-tuple-element.53), channel_id=1, replica_groups=mesh['tile'=8,'grp'=32] {'tile'}, use_global_device_ids=true, to_apply=%region_5.6 | all-reduce | flops 132 | bytes 1056 | tf_op jit(solution)/shard_map/psum | solution.py:125
  429.6 54.0 %psum.59 = f32[2,528]{1,0:T(2,128)S(1)} all-reduce(f32[2,528]{1,0:T(2,128)S(1)} %fusion.57), channel_id=1, replica_groups=mesh['tile'=8,'grp'=32] {'grp'}, use_global_device_ids=true, to_apply=%region_6.7 | all-reduce | flops 1056 | bytes 8448 | tf_op jit(solution)/shard_map/psum | solution.py:129
  486.7 2.1 collective-permute-start.4
  505.0 4.3 reshape.179
  509.4 2.0 fusion.60
  515.2 4.8 fusion.63
  520.0 5.6 collective-permute-done.6
  525.6 2.0 bitcast_add_fusion
  529.0 4.0 fusion.62
  534.3 4.0 convolution_bitcast_fusion.1
  538.3 3.4 fusion.3
  541.8 69.2 %fusion.1 = bf16[72,1024]{1,0:T(8,128)(2,1)S(1)} fusion(bf16[2112,1024]{1,0:T(8,128)(2,1)} %fusion.3), kind=kCustom, calls=%all-reduce-scatter.1 | all-reduce-scatter fusion | flops 2359297 | bytes 4473856
  611.0 1.9 collective-permute-start.11
  613.0 1.9 collective-permute-start.12
  614.9 1.9 collective-permute-start.13
  617.9 8.4 %collective-permute-done.13 = bf16[42,1024]{1,0:T(8,128)(2,1)S(1)} collective-permute-done((bf16[42,1024]{1,0:T(8,128)(2,1)S(1)}, bf16[42,1024]{1,0:T(8,128)(2,1)S(1)}, u32[]{:S(2)}, u32[]{:S(2)}) %collective-permute-start.13) | collective-permute-done | bytes 86048
  627.9 2.5 all-reduce.12.cloned.1.call-done
  630.5 4.3 convolution_bitcast_fusion
  637.8 2.7 copy.136
  641.7 2.9 fusion.5
  644.6 115.2 %all-reduce.10.cloned.1.call-done = f32[256,2112]{0,1:T(8,128)} async-done(((f32[256,2112]{0,1:T(8,128)}), f32[256,2112]{0,1:T(8,128)}) %all-reduce.10.cloned.1.call-update) | async-done | bytes 2162704 | tf_op jit(solution)/shard_map/psum | solution.py:157
  759.8 4.5 fusion.6
  (140 shorter events, 63.3 us)
Async XLA Ops:
  7.2 633.3 %copy-start = (f32[2112,256]{1,0:T(8,128)S(1)}, f32[2112,256]{1,0:T(8,128)}, u32[]{:S(2)}) copy-start(f32[2112,256]{1,0:T(8,128)} %param.24) | copy-start | bytes 6488068
  7.2 65.6 %all-gather.3.cloned.1.call-start = ((), (), s32[]{:S(2)}) async-start(), calls=%async_computation | async-start | bytes 8921088 | tf_op jit(solution)/shard_map/all_gather | solution.py:69
  9.3 74.8 %copy-start.12 = (bf16[2112,66]{0,1:T(8,128)(2,1)S(1)}, bf16[2112,66]{0,1:T(8,128)(2,1)}, u32[]{:S(2)}) copy-start(bf16[2112,66]{0,1:T(8,128)(2,1)} %param.15) | copy-start | bytes 836356
  9.3 74.8 %copy-start.23 = (f32[66]{0:T(128)S(1)}, f32[66]{0:T(128)}, u32[]{:S(2)}) copy-start(f32[66]{0:T(128)} %param.16) | copy-start | bytes 796
  9.3 387.3 %all-gather.5.cloned.1.call-start = ((), (), s32[]{:S(2)}) async-start(), calls=%async_computation.1 | async-start | bytes 8921088 | tf_op jit(solution)/shard_map/all_gather | solution.py:117
  88.8 1.6 collective-permute-start
  90.7 15.6 %copy-start.1 = (bf16[2,8,64,132]{2,1,0,3:T(8,128)(2,1)}, bf16[2,8,64,132]{2,1,0,3:T(8,128)(2,1)S(1)}, u32[]{:S(2)}) copy-start(bf16[2,8,64,132]{2,1,0,3:T(8,128)(2,1)S(1)} %maximum_select_fusion.2) | copy-start | bytes 811012
  92.0 14.3 %collective-permute-start.1 = (bf16[2,8,64,132]{3,2,1,0:T(8,128)(2,1)}, bf16[2,8,64,132]{3,2,1,0:T(8,128)(2,1)S(1)}, u32[]{:S(2)}, u32[]{:S(2)}) collective-permute-start(bf16[2,8,64,132]{3,2,1,0:T(8,128)(2,1)} %copy.117), channel_id=1, source_target_pairs={{0,2},{1,3},{2,0},{3,1},{4,6},{5,7},{6,4},{7,5},{8,10},{9,11},{10,... | collective-permute-start | bytes 811016 | tf_op jit(solution)/shard_map/ppermute | solution.py:12
  110.8 12.1 %collective-permute-start.2 = (bf16[2,1,64,264]{2,1,0,3:T(2,128)(2,1)}, bf16[2,1,64,264]{2,1,0,3:T(2,128)(2,1)}, u32[]{:S(2)}, u32[]{:S(2)}) collective-permute-start(bf16[2,1,64,264]{2,1,0,3:T(2,128)(2,1)} %get-tuple-element.45), channel_id=1, source_target_pairs={{0,32},{32,64},{64,96},{96,128},{128,160},{160,192},{192,224},{1,3... | collective-permute-start | bytes 202760 | tf_op jit(solution)/shard_map/ppermute | solution.py:22
  115.0 9.6 %collective-permute-start.3 = (bf16[2,1,64,264]{2,1,0,3:T(2,128)(2,1)}, bf16[2,1,64,264]{2,1,0,3:T(2,128)(2,1)S(1)}, u32[]{:S(2)}, u32[]{:S(2)}) collective-permute-start(bf16[2,1,64,264]{2,1,0,3:T(2,128)(2,1)} %get-tuple-element.46), channel_id=1, source_target_pairs={{32,0},{64,32},{96,64},{128,96},{160,128},{192,160},{224,192},{33,... | collective-permute-start | bytes 202760 | tf_op jit(solution)/shard_map/ppermute | solution.py:23
  131.9 2.7 copy-start.2
  131.9 2.7 copy-start.3
  142.2 13.6 %copy-start.6 = (bf16[66,2376]{1,0:T(8,128)(2,1)S(1)}, bf16[66,2376]{1,0:T(8,128)(2,1)}, u32[]{:S(2)}) copy-start(bf16[66,2376]{1,0:T(8,128)(2,1)} %reshape.165) | copy-start | bytes 940900
  142.2 13.6 %copy-start.21 = (f32[66]{0:T(128)S(1)}, f32[66]{0:T(128)}, u32[]{:S(2)}) copy-start(f32[66]{0:T(128)} %param.18) | copy-start | bytes 796
  155.8 21.2 %copy-start.19 = (bf16[66,528]{1,0:T(8,128)(2,1)S(1)}, bf16[66,528]{1,0:T(8,128)(2,1)}, u32[]{:S(2)}) copy-start(bf16[66,528]{1,0:T(8,128)(2,1)} %param.19) | copy-start | bytes 209092
  155.9 75.4 %copy-start.17 = (bf16[528,66]{0,1:T(8,128)(2,1)S(1)}, bf16[528,66]{0,1:T(8,128)(2,1)}, u32[]{:S(2)}) copy-start(bf16[528,66]{0,1:T(8,128)(2,1)} %param.21) | copy-start | bytes 209092
  155.9 75.4 %copy-start.20 = (f32[528]{0:T(1024)S(1)}, f32[528]{0:T(1024)}, u32[]{:S(2)}) copy-start(f32[528]{0:T(1024)} %param.20) | copy-start | bytes 6340
  155.9 75.3 %copy-start.24 = (f32[66]{0:T(128)S(1)}, f32[66]{0:T(128)}, u32[]{:S(2)}) copy-start(f32[66]{0:T(128)} %param.22) | copy-start | bytes 796
  236.4 76.9 %copy-start.4 = (f32[1024,66]{1,0:T(8,128)S(1)}, f32[1024,66]{1,0:T(8,128)}, u32[]{:S(2)}) copy-start(f32[1024,66]{1,0:T(8,128)} %bitcast_convert_fusion.1) | copy-start | bytes 811012
  236.4 79.0 %copy-start.22 = (u32[256]{0:T(256)S(1)}, u32[256]{0:T(256)}, u32[]{:S(2)}) copy-start(u32[256]{0:T(256)} %constant.52) | copy-start | bytes 3076
  305.5 15.6 %collective-permute-start.8 = (bf16[72,1024]{1,0:T(8,128)(2,1)S(1)}, bf16[72,1024]{1,0:T(8,128)(2,1)S(1)}, u32[]{:S(2)}, u32[]{:S(2)}) collective-permute-start(bf16[72,1024]{1,0:T(8,128)(2,1)S(1)} %fusion), channel_id=1, source_target_pairs={{0,1},{1,2},{2,3},{3,4},{4,5},{5,6},{6,7},{7,8},{8,9},{9,10},{10,1... | collective-permute-start | bytes 442376
  307.4 13.7 %collective-permute-start.9 = (bf16[72,1024]{1,0:T(8,128)(2,1)S(1)}, bf16[72,1024]{1,0:T(8,128)(2,1)}, u32[]{:S(2)}, u32[]{:S(2)}) collective-permute-start(bf16[72,1024]{1,0:T(8,128)(2,1)S(1)} %fusion), channel_id=1, source_target_pairs={{0,2},{1,3},{2,4},{3,5},{4,6},{5,7},{6,8},{7,9},{8,10},{9,11},{10,... | collective-permute-start | bytes 442376
  309.4 11.8 %collective-permute-start.10 = (bf16[42,1024]{1,0:T(8,128)(2,1)}, bf16[42,1024]{1,0:T(8,128)(2,1)S(1)}, u32[]{:S(2)}, u32[]{:S(2)}) collective-permute-start(bf16[42,1024]{1,0:T(8,128)(2,1)} %slice.132), channel_id=1, source_target_pairs={{0,3},{1,4},{2,5},{3,6},{4,7},{5,8},{6,9},{7,10},{8,11},{9,12},{10... | collective-permute-start | bytes 258056
  328.2 79.7 %copy-start.7 = (bf16[1024,66]{0,1:T(8,128)(2,1)}, bf16[1024,66]{0,1:T(8,128)(2,1)S(1)}, u32[]{:S(2)}) copy-start(bf16[1024,66]{0,1:T(8,128)(2,1)S(1)} %get-tuple-element.47) | copy-start | bytes 405508
  329.2 301.3 %all-reduce.12.cloned.1.call-start = ((), (), s32[]{:S(2)}) async-start(), calls=%async_computation.3 | async-start | bytes 3907584 | tf_op jit(solution)/shard_map/psum | solution.py:150
  407.9 21.5 %copy-start.18 = (bf16[528,66]{0,1:T(8,128)(2,1)S(1)}, bf16[528,66]{0,1:T(8,128)(2,1)}, u32[]{:S(2)}) copy-start(bf16[528,66]{0,1:T(8,128)(2,1)} %param.21) | copy-start | bytes 209092
  407.9 82.1 %copy-start.5 = (bf16[66,9,264]{2,0,1:T(8,128)(2,1)S(1)}, bf16[66,9,264]{2,0,1:T(8,128)(2,1)}, u32[]{:S(2)}) copy-start(bf16[66,9,264]{2,0,1:T(8,128)(2,1)} %param.17) | copy-start | bytes 940900
  484.9 0.7 copy-start.9
  485.6 5.3 copy-start.10
  486.7 7.5 collective-permute-start.4
  488.7 6.5 collective-permute-start.5
  512.2 13.4 %collective-permute-start.6 = (f32[1024,132]{0,1:T(8,128)}, f32[1024,132]{0,1:T(8,128)}, u32[]{:S(2)}, u32[]{:S(2)}) collective-permute-start(f32[1024,132]{0,1:T(8,128)} %select_bitcast_fusion), channel_id=1, source_target_pairs={{0,2},{1,3},{2,0},{3,1},{4,6},{5,7},{6,4},{7,5},{8,10},{9,11},{10,... | collective-permute-start | bytes 1622024 | tf_op jit(solution)/shard_map/ppermute | solution.py:12
  528.7 5.4 collective-permute-start.7
  529.0 5.1 copy-start.16
  534.3 4.0 copy-start.13
  541.7 85.3 %copy-start.8 = (bf16[1024,66]{0,1:T(8,128)(2,1)S(1)}, bf16[1024,66]{0,1:T(8,128)(2,1)}, u32[]{:S(2)}) copy-start(bf16[1024,66]{0,1:T(8,128)(2,1)} %copy-done.7) | copy-start | bytes 405508
  541.8 88.7 %copy-start.14 = (f32[66,256]{1,0:T(8,128)S(1)}, f32[66,256]{1,0:T(8,128)}, u32[]{:S(2)}) copy-start(f32[66,256]{1,0:T(8,128)} %param.25) | copy-start | bytes 202756
  541.8 218.1 %all-reduce.10.cloned.1.call-start = ((), (), s32[]{:S(2)}) async-start(), calls=%async_computation.2 | async-start | bytes 4325376 | tf_op jit(solution)/shard_map/psum | solution.py:157
  611.0 15.2 %collective-permute-start.11 = (bf16[72,1024]{1,0:T(8,128)(2,1)S(1)}, bf16[72,1024]{1,0:T(8,128)(2,1)S(1)}, u32[]{:S(2)}, u32[]{:S(2)}) collective-permute-start(bf16[72,1024]{1,0:T(8,128)(2,1)S(1)} %fusion.1), channel_id=1, source_target_pairs={{0,1},{1,2},{2,3},{3,4},{4,5},{5,6},{6,7},{7,8},{8,9},{9,10},{10,1... | collective-permute-start | bytes 442376
  613.0 13.3 %collective-permute-start.12 = (bf16[72,1024]{1,0:T(8,128)(2,1)S(1)}, bf16[72,1024]{1,0:T(8,128)(2,1)S(1)}, u32[]{:S(2)}, u32[]{:S(2)}) collective-permute-start(bf16[72,1024]{1,0:T(8,128)(2,1)S(1)} %fusion.1), channel_id=1, source_target_pairs={{0,2},{1,3},{2,4},{3,5},{4,6},{5,7},{6,8},{7,9},{8,10},{9,11},{10,... | collective-permute-start | bytes 442376
  614.9 11.4 %collective-permute-start.13 = (bf16[42,1024]{1,0:T(8,128)(2,1)S(1)}, bf16[42,1024]{1,0:T(8,128)(2,1)S(1)}, u32[]{:S(2)}, u32[]{:S(2)}) collective-permute-start(bf16[42,1024]{1,0:T(8,128)(2,1)S(1)} %slice.133), channel_id=1, source_target_pairs={{0,3},{1,4},{2,5},{3,6},{4,7},{5,8},{6,9},{7,10},{8,11},{9,12},{10... | collective-permute-start | bytes 258056
  636.0 4.5 copy-start.11
  640.4 119.4 %copy-start.15 = (f32[66,256]{1,0:T(8,128)S(1)}, f32[66,256]{1,0:T(8,128)}, u32[]{:S(2)}) copy-start(f32[66,256]{1,0:T(8,128)} %param.25) | copy-start | bytes 202756
Sparse Core Ops, SparseCore 0:
  11.1 61.5 all-gather.2
  329.3 67.2 all-gather.4
  541.9 88.5 all-reduce.11
  634.9 124.8 all-reduce.9
where the time goes:
time: 779 us; the launch traced here: 771 us
  waiting for transfers between devices  285 us (37%)
  blocking collectives  280 us (36%)
  local copies, waits for them, and re-layouts  91.3 us (12%)
  matrix products  51.3 us (7%)
  other arithmetic  25.8 us (3%)
  starting transfers between devices  21.9 us (3%)
  between operations  15.2 us (2%)
    unnamed x2, blocking collectives  138 us
    psum x1, waiting for transfers between devices, per_device(): lax.psum(jnp.dot(second_basis.T, second_sum, precision=highest), 'grp')  115 us
    all_gather x1, waiting for transfers between devices, per_device(): lax.all_gather(back.reshape(images, rows_dev, col_count, ch_dev), 'grp',...  67.4 us
    all_gather x1, waiting for transfers between devices, per_device(): everything = lax.all_gather(inputs, 'grp', axis=3, tiled=True)  63.4 us
    psum x1, blocking collectives, per_device(): lax.psum(jnp.dot(means, squeeze_matrix, precision=highest), 'grp')  54 us
    psum x1, blocking collectives, per_device(): squeeze_back = lax.psum(squeeze_part, 'grp') * slope(squeeze_pre)  54 us
    unnamed x77, local copies, waits for them, and re-layouts  29.7 us
    ppermute x4, waiting for transfers between devices, swapped(): lax.ppermute(shard, axis, [(i, i ^ 1 << apart) for i in range(lax.axis_si...  21 us
  transfers between devices with their start and end apart: 18, of which 11 were waited for; matrix products, arithmetic and copies ran while one was open for 14% of the time, Pallas kernels for 0%

commit v1 on v0

v1 whole, which is shorter than its diff:
```python
import math

import jax
import jax.numpy as jnp
from jax import lax
from jax.experimental import pallas as pl
from jax.experimental.pallas import tpu as pltpu
from jax.sharding import PartitionSpec as P

MESH = pl.DeviceIdType.MESH
highest = lax.Precision.HIGHEST
bf16, f32 = jnp.bfloat16, jnp.float32

TILES = 8
GRP = 32
CH_DEV = 66
CB = 80
PX = 256
GP = 4 * CB
AP = GRP * CB
CI = 272
SQ = 528
SQP = 640
BASIS = 256
ZC = 384
CELLS = 4096.0
NSEM = 240


def flip(index, mask):
    out = index
    for bit in range(5):
        if mask >> bit & 1:
            step = 1 << bit
            out = out + step * (1 - 2 * ((index // step) % 2))
    return out


def sigmoid(v):
    return 1.0 / (1.0 + jnp.exp(-v))


def slope(v):
    sig = sigmoid(v)
    return sig * (1.0 + v * (1.0 - sig))


def dot(a, b):
    return lax.dot_general(a, b, (((1,), (0,)), ((), ())), preferred_element_type=f32)


def dot_nt(a, b):
    return lax.dot_general(a, b, (((1,), (1,)), ((), ())), preferred_element_type=f32)


def pieces(v, count):
    out = []
    for _ in range(count - 1):
        top = v.astype(bf16)
        out.append(top)
        v = v - top.astype(f32)
    out.append(v.astype(bf16))
    return out


def split_left(op, a, b, count=3):
    return sum(op(p, b) for p in pieces(a, count))


def split_right(op, a, b, count=3):
    return sum(op(a, p) for p in pieces(b, count))


def body(
    xq, cq, w1, wc, w2, sm, fp, fbt, sqb,
    bo, ig, zo, sg, se,
    xall, ball, w1g, wcg, w2g, w1t, wct, w2t, smg, fpg,
    ext, extg, ext2, cols, pre, conv_out, hidden, sback, xbt, sbt, zbuf,
    rs_send, rs_own, rs_recv, rs2_send, rs2_recv, bq,
    usend, urecv, c2s, c2r, c2z, c2zr, c2all,
    hs, hz, hb8, es, ez, eb8, hbs, hbr, c1s, c1r, zs, zf, zr, zall,
    send, recv, local,
):
    z = lax.axis_index("tile")
    me = lax.axis_index("grp")
    xx = me // 8
    col = me % 8
    m = me % 4
    g = me // 4
    core = me % 2
    img = (me // 2) % 2
    count = [0]
    started = []
    locals_ = []

    def copy(src, dst, tile, grp):
        i = count[0]
        count[0] += 1
        c = pltpu.make_async_remote_copy(
            src_ref=src, dst_ref=dst, send_sem=send.at[i], recv_sem=recv.at[i],
            device_id=(tile, grp), device_id_type=MESH,
        )
        c.start()
        started.append(c)
        return c

    def keep(src, dst):
        c = pltpu.make_async_copy(src, dst, local.at[len(locals_)])
        c.start()
        locals_.append(c)
        return c

    def peer(mask):
        return flip(me, mask)

    other = (lax.rem(z + 2 * core - 1 + TILES, TILES), flip(me, 1))
    grp_masks = [1, 2, 3, 4, 5, 6, 7, 8, 16, 24, 12, 20, 28]
    g_masks = [4, 8, 12, 16, 20, 24, 28]

    barrier = pltpu.get_barrier_semaphore()
    for mask in grp_masks:
        pl.semaphore_signal(barrier, inc=1, device_id=(z, peer(mask)), device_id_type=MESH)
    for mask in range(1, 8):
        pl.semaphore_signal(barrier, inc=1, device_id=(flip(z, mask), me), device_id_type=MESH)
    pl.semaphore_signal(barrier, inc=1, device_id=other, device_id_type=MESH)
    pl.semaphore_wait(barrier, len(grp_masks) + 8)

    def gather_column(pick, dst, slot):
        return [copy(pick(k), dst.at[slot(0)], z, peer(k)) for k in range(1, 8)]

    def gather_rows(arrived, dst, slot):
        done = []
        for k in range(8):
            if k:
                arrived[k - 1].wait_recv()
            for mask in (8, 16, 24):
                done.append(copy(dst.at[slot(k)], dst.at[slot(k)], z, peer(mask)))
        return done

    def group_start(src, dst):
        mine = keep(src, dst.at[m])
        return mine, copy(src, dst.at[m], z, peer(1)), copy(src, dst.at[m], z, peer(2))

    def group_forward(state, dst):
        mine, near, far = state
        far.wait_recv()
        slot = flip(m, 2)
        return mine, near, copy(dst.at[slot], dst.at[slot], z, peer(1))

    def group_finish(state):
        state[0].wait()
        state[1].wait_recv()
        state[2].wait_recv()

    def halo_start(buf):
        return (
            copy(buf.at[2 - core], buf.at[3 * core], z, peer(1)),
            copy(buf.at[1 + core], buf.at[3 - 3 * core], other[0], other[1]),
        )

    def halo_finish(buf, copies):
        for c in copies:
            c.wait_recv()

        @pl.when((z == 0) & (core == 0))
        def _():
            buf[0] = jnp.zeros(buf.shape[1:], buf.dtype)

        @pl.when((z == TILES - 1) & (core == 1))
        def _():
            buf[3] = jnp.zeros(buf.shape[1:], buf.dtype)

    def wide(buf):
        return jnp.concatenate([buf[0], buf[1], buf[2], buf[3]], axis=1)

    def block(k):
        return flip(me, k)

    xs = gather_column(lambda k: xq.at[flip(m, k & 3)], xall, block)
    s1 = group_start(w1, w1g)
    sc = group_start(wc, wcg)
    ssm = group_start(sm, smg)
    sfp = group_start(fp, fpg)
    s2 = group_start(w2, w2g)
    keep(xq.at[m], xall.at[me]).wait()
    xrows = gather_rows(xs, xall, block)
    s1 = group_forward(s1, w1g)
    sfp_ = group_forward(sfp, fpg)

    row = lax.broadcasted_iota(jnp.int32, (CI, GP), 0)
    lane = lax.broadcasted_iota(jnp.int32, (CI, GP), 1)
    shifted = row
    for part in (1, 2, 3):
        shifted = shifted + jnp.where(row >= CH_DEV * part, CB - CH_DEV, 0)
    pack = jnp.where((shifted == lane) & (row < 4 * CH_DEV), 1.0, 0.0).astype(bf16)
    row_t = lax.broadcasted_iota(jnp.int32, (GP, CI), 1)
    lane_t = lax.broadcasted_iota(jnp.int32, (GP, CI), 0)
    shifted_t = row_t
    for part in (1, 2, 3):
        shifted_t = shifted_t + jnp.where(row_t >= CH_DEV * part, CB - CH_DEV, 0)
    unpack = jnp.where((shifted_t == lane_t) & (row_t < 4 * CH_DEV), 1.0, 0.0).astype(bf16)

    group_finish(s1)
    group_finish(sfp_)
    for c in xrows:
        c.wait_recv()

    x_rows = xall[...].reshape(AP, PX)
    first_pre = dot(w1g[...].reshape(GP, AP), x_rows) + fpg[...].reshape(GP, 384)[:, 0:1]
    active = (first_pre * sigmoid(first_pre)).astype(bf16)
    packed = dot(pack, active).astype(bf16)
    ext[1] = packed[:, 0:128]
    ext[2] = packed[:, 128:256]
    halo = halo_start(ext)
    pre[...] = split_right(dot, pack, first_pre)
    sc = group_forward(sc, wcg)
    ssm = group_forward(ssm, smg)
    s2 = group_forward(s2, w2g)

    cols[...] = jnp.zeros(cols.shape, bf16)

    def build(read, target):
        lanes = lax.broadcasted_iota(jnp.int32, (16, 512), 1) % 64

        def step(i, carry):
            r = pl.multiple_of(i * 16, 16)
            e = jnp.concatenate([read(n, r) for n in range(4)], axis=1).astype(f32)
            for b in (-1, 0, 1):
                if b == 0:
                    v = e
                elif b == 1:
                    v = jnp.where(lanes == 63, 0.0, pltpu.roll(e, 511, 1))
                else:
                    v = jnp.where(lanes == 0, 0.0, pltpu.roll(e, 1, 1))
                s = pltpu.roll(v, 64, 1)
                for a, win in ((-1, s[:, 128:384]), (0, v[:, 128:384]), (1, s[:, 256:512])):
                    t = 3 * (a + 1) + b + 1
                    target[pl.ds(pl.multiple_of(t * CI + r, 16), 16), :] = win.astype(bf16)
            return carry

        lax.fori_loop(0, CI // 16, step, 0)

    halo_finish(ext, halo)
    sext = group_start(ext, extg)
    build(lambda n, r: ext[n, pl.ds(r, 16), :], cols)
    group_finish(sc)

    co = dot(wcg[...].reshape(GP, AP), cols[...]) + fpg[...].reshape(GP, 384)[:, 1:2]
    conv_out[...] = co
    hid = co * sigmoid(co)
    hidden[...] = hid
    ones = jnp.ones((8, PX), bf16)
    images = lax.broadcasted_iota(jnp.int32, (8, GP), 0)

    def sums_start(v, buf):
        buf[0] = jnp.zeros((8, 384), f32)
        buf[0, :, 0:GP] = jnp.where(images == img, split_right(dot_nt, ones, v), 0.0)
        return [copy(buf.at[0], buf.at[k], z, peer(k)) for k in range(1, 4)]

    def sums_tiles(copies, buf, wider):
        for c in copies:
            c.wait_recv()
        wider[0] = buf[0] + buf[1] + buf[2] + buf[3]
        return [copy(wider.at[0], wider.at[k], flip(z, k), me) for k in range(1, 8)]

    def sums_finish(copies, wider):
        for c in copies:
            c.wait_recv()
        return sum(wider[k] for k in range(8))[:, 0:GP]

    def squeeze_start(v, buf):
        buf[0] = v
        return [copy(buf.at[0], buf.at[n + 1], z, peer(k)) for n, k in enumerate(g_masks)]

    def squeeze_finish(copies, buf):
        for c in copies:
            c.wait_recv()
        return sum(buf[n] for n in range(8))

    ah = sums_start(hid, hs)

    def transposed(src, dst):
        def step(j, carry):
            at = pl.multiple_of(j * 128, 128)
            v = src[:, :, pl.ds(at, 128)].reshape(GP, 128)
            dst[pl.ds(at, 128), :] = v.T
            return carry

        lax.fori_loop(0, AP // 128, step, 0)

    sh = sums_tiles(ah, hs, hz)
    group_finish(ssm)
    group_finish(s2)
    transposed(w2g, w2t)
    sb = fpg[...].reshape(GP, 384)[:, 128:384]
    sb_top = sb.astype(bf16)
    sbt[0:BASIS, :] = sb_top.T
    sbt[BASIS:, :] = (sb - sb_top.astype(f32)).astype(bf16).T
    means = sums_finish(sh, hz) * (1.0 / CELLS)
    sq_w = smg[:, :, 0:SQP].reshape(GP, SQP)
    ex_w = smg[:, :, SQP:].reshape(GP, SQP)
    bh = squeeze_start(split_left(dot, means, sq_w), hb8)
    sext = group_forward(sext, extg)
    xb2 = dot(fbt[...], x_rows)
    xb = xb2[0:BASIS] + xb2[BASIS:]
    xb_top = xb.astype(bf16)
    xbt[0:BASIS, :] = xb_top
    xbt[BASIS:, :] = (xb - xb_top.astype(f32)).astype(bf16)
    squeeze_pre = squeeze_finish(bh, hb8) + sqb[...]
    squeeze = squeeze_pre * sigmoid(squeeze_pre)
    ex_logit = split_right(dot_nt, ex_w, squeeze) + fpg[...].reshape(GP, 384)[:, 2:3]
    excite = sigmoid(ex_logit)
    ex_col = jnp.where(img == 0, excite[:, 0:1], excite[:, 1:2])
    scaled = (hidden[...] * ex_col).astype(bf16)

    def reduce_start(left, right, inner):
        out = []
        for k in (3, 2, 1, 0):
            at = pl.multiple_of(flip(xx, k) * (8 * CB), 128)
            p = dot(left[pl.ds(at, 8 * CB), :], right)
            if k:
                rs_send[inner, k] = p.astype(bf16).reshape(8, CB, PX)
                out.append(copy(rs_send.at[inner, k], rs_recv.at[inner, k], z, peer(8 * k)))
            else:
                rs_own[...] = p
        return out

    def reduce_column(copies, inner):
        for c in copies:
            c.wait_recv()
        total = rs_own[...]
        for k in (1, 2, 3):
            total = total + rs_recv[inner, k].reshape(8 * CB, PX).astype(f32)
        rs2_send[inner] = total.astype(bf16).reshape(8, CB, PX)
        return [
            copy(rs2_send.at[inner, flip(col, k)], rs2_recv.at[inner, k], z, peer(k))
            for k in range(1, 8)
        ]

    def reduce_quarter(copies, inner, kk):
        copies[kk + 3].wait_recv()
        if kk:
            copies[kk - 1].wait_recv()
            first = rs2_recv[inner, kk]
        else:
            first = rs2_send[inner, col]
        return first.astype(f32) + rs2_recv[inner, kk + 4].astype(f32)

    r1 = reduce_start(w2t, scaled, 0)
    u2 = dot(sbt[...], scaled)
    usend[...] = (u2[0:BASIS] + u2[BASIS:]).astype(bf16).reshape(8, 32, PX)
    us = [copy(usend.at[flip(g, k // 4)], urecv.at[n + 1], z, peer(k)) for n, k in enumerate(g_masks)]
    transposed(w1g, w1t)
    transposed(wcg, wct)
    c2cols = reduce_column(r1, 0)
    back_copies = [None] * 7
    for kk in range(4):
        q = flip(m, kk)
        total = xq[q].astype(f32) + reduce_quarter(c2cols, 0, kk)
        sig = sigmoid(total)
        bo[q] = (total * sig).astype(bf16)
        bq[q] = (cq[q].astype(f32) * (sig * (1.0 + total * (1.0 - sig)))).astype(bf16)
        for k in (kk, kk + 4):
            if k:
                back_copies[k - 1] = copy(bq.at[q], ball.at[me], z, peer(k))
    ball[me] = bq[m]
    brows = gather_rows(back_copies, ball, block)
    group_finish(sext)
    for c in us:
        c.wait_recv()
    u_own = usend[g].astype(f32)
    for n in range(1, 8):
        u_own = u_own + urecv[n].astype(f32)
    u_top = u_own.astype(bf16)
    u_low = (u_own - u_top.astype(f32)).astype(bf16)
    for c in brows:
        c.wait_recv()

    back_rows = ball[...].reshape(AP, PX)
    scaled_back = dot(w2g[...].reshape(GP, AP), back_rows)
    sback[...] = scaled_back
    ae = sums_start(scaled_back * hidden[...], es)
    coords = dot_nt(u_top, back_rows) + dot_nt(u_low, back_rows)
    se_ = sums_tiles(ae, es, ez)
    for k in range(4):
        c2s[k] = coords[:, 640 * k : 640 * (k + 1)].astype(bf16)
    c2g = [copy(c2s.at[flip(m, k)], c2r.at[k], z, peer(k)) for k in range(1, 4)]
    ex_row = sigmoid(
        split_left(dot_nt, squeeze, ex_w)
        + split_right(
            dot_nt,
            jnp.where(lax.broadcasted_iota(jnp.int32, (8, 128), 1) == 2, 1.0, 0.0).astype(bf16),
            fpg[...].reshape(GP, 384)[:, 0:128],
        )
    )
    excite_back = sums_finish(se_, ez)
    sig_back = excite_back * ex_row * (1.0 - ex_row)
    be = squeeze_start(split_left(dot, sig_back, ex_w), eb8)
    for c in c2g:
        c.wait_recv()
    c2 = c2s[m].astype(f32) + c2r[1].astype(f32) + c2r[2].astype(f32) + c2r[3].astype(f32)
    c2z[...] = c2.astype(bf16)
    c2t = [copy(c2z, c2zr.at[k], flip(z, k), me) for k in range(1, 8)]
    squeeze_back = squeeze_finish(be, eb8) * slope(squeeze_pre)
    means_back = split_right(dot_nt, sq_w, squeeze_back)
    mb_col = jnp.where(img == 0, means_back[:, 0:1], means_back[:, 1:2]) * (1.0 / CELLS)
    hb = ((sback[...] * ex_col + mb_col) * slope(conv_out[...])).astype(bf16)
    ext2[1] = hb[:, 0:128]
    ext2[2] = hb[:, 128:256]
    halo2 = halo_start(ext2)
    hbs[...] = hb.reshape(4, CB, PX)
    hsw = [copy(hbs.at[flip(m, k)], hbr.at[k], z, peer(k)) for k in range(1, 4)]
    se[0] = jnp.zeros((8, SQP), f32)
    se[1] = jnp.zeros((8, SQP), f32)
    se[0, :, 0:GP] = means
    se[1, :, 0:GP] = sig_back
    se[2] = squeeze
    se[3] = squeeze_back

    for c in c2t:
        c.wait_recv()
    c2 = c2z[...].astype(f32)
    for k in range(1, 8):
        c2 = c2 + c2zr[k].astype(f32)

    def slot2(k):
        return flip(m, k & 3) * 8 + flip(g, k >> 2)

    c2all[slot2(0)] = c2.astype(bf16)
    c2c = gather_column(lambda k: c2all.at[slot2(0)], c2all, slot2)
    halo_finish(ext2, halo2)

    zbuf[...] = dot(wct[...], wide(ext2))
    lanes8 = lax.broadcasted_iota(jnp.int32, (16, PX), 1) % 64

    def gathered(i, carry):
        r = pl.multiple_of(i * 16, 16)
        acc = jnp.zeros((16, PX), f32)
        for b in (-1, 0, 1):
            up = zbuf[pl.ds(pl.multiple_of(CI * (b + 1) + r, 16), 16), :]
            mid = zbuf[pl.ds(pl.multiple_of(CI * (b + 4) + r, 16), 16), :]
            down = zbuf[pl.ds(pl.multiple_of(CI * (b + 7) + r, 16), 16), :]
            y = mid[:, 128:384] + pltpu.roll(up, 64, 1)[:, 256:512] + pltpu.roll(down, 64, 1)[:, 128:384]
            if b == 1:
                y = jnp.where(lanes8 == 0, 0.0, pltpu.roll(y, 1, 1))
            elif b == -1:
                y = jnp.where(lanes8 == 63, 0.0, pltpu.roll(y, PX - 1, 1))
            acc = acc + y
        pre[pl.ds(r, 16), :] = acc * slope(pre[pl.ds(r, 16), :])
        return carry

    lax.fori_loop(0, CI // 16, gathered, 0)
    ag = dot(unpack, pre[...].astype(bf16)).astype(bf16)
    r2 = reduce_start(w1t, ag, 1)
    c2rows = gather_rows(c2c, c2all, slot2)

    c1 = dot_nt(ag, xbt[0:BASIS, :]) + dot_nt(ag, xbt[BASIS:, :])
    c1s[...] = c1.astype(bf16).reshape(4, CB, BASIS)
    c1g = [copy(c1s.at[flip(m, k)], c1r.at[k], z, peer(k)) for k in range(1, 4)]
    for c in hsw:
        c.wait_recv()
    grads = dot_nt(hbs[m], cols[...])
    for k in range(1, 4):
        q = flip(m, k)
        build(lambda n, r: extg[q, n, pl.ds(r, 16), :], cols)
        grads = grads + dot_nt(hbr[k], cols[...])
    for c in c1g:
        c.wait_recv()
    c1 = c1s[m].astype(f32) + c1r[1].astype(f32) + c1r[2].astype(f32) + c1r[3].astype(f32)
    both = jnp.concatenate([grads, c1, jnp.zeros((CB, TILES * ZC - AP - BASIS), f32)], axis=1)
    for k in range(TILES):
        zf[k] = both[:, ZC * k : ZC * (k + 1)]
        zs[k] = both[:, ZC * k : ZC * (k + 1)].astype(bf16)
    z1 = [copy(zs.at[flip(z, k)], zr.at[k], flip(z, k), me) for k in range(1, 8)]
    c2cols = reduce_column(r2, 1)
    for c in z1:
        c.wait_recv()
    chunk = zf[z]
    for k in range(1, 8):
        chunk = chunk + zr[k].astype(f32)
    zall[z] = chunk.astype(bf16)
    z2 = [copy(zall.at[z], zall.at[z], flip(z, k), me) for k in range(1, 8)]
    for kk in range(4):
        q = flip(m, kk)
        ig[q] = (bq[q].astype(f32) + reduce_quarter(c2cols, 1, kk)).astype(bf16)
    for c in c2rows:
        c.wait_recv()
    own = fp[:, 128:384]
    own_top = own.astype(bf16)
    own_low = (own - own_top.astype(f32)).astype(bf16)
    for k in range(4):
        rows = c2all[8 * k : 8 * (k + 1)].reshape(BASIS, 640)
        sg[:, 640 * k : 640 * (k + 1)] = dot(own_top, rows) + dot(own_low, rows)
    for c in z2:
        c.wait_recv()
    zo[...] = zall[...]
    for c in started:
        c.wait_send()


def per_device(
    inputs,
    cotangent,
    first_weight,
    first_bias,
    conv_weight,
    conv_bias,
    squeeze_weight,
    squeeze_bias,
    excite_weight,
    excite_bias,
    second_weight,
    first_basis,
    second_basis,
):
    grad_scale = 1.0 / math.sqrt(8192.0)

    def quarters(v):
        v = v.reshape(2, 2, PX, CH_DEV).transpose(0, 1, 3, 2)
        return jnp.pad(v, ((0, 0), (0, 0), (0, CB - CH_DEV), (0, 0))).reshape(4, CB, PX)

    def spread(v):
        v = v.reshape(CH_DEV, GRP, CH_DEV)
        return jnp.pad(v, ((0, CB - CH_DEV), (0, 0), (0, CB - CH_DEV))).reshape(CB, AP)

    xq, cq = quarters(inputs), quarters(cotangent)
    w1 = spread(first_weight.T)
    w2 = spread(second_weight)
    wc = jnp.pad(conv_weight, ((0, CB - CH_DEV), (0, 0), (0, CI - 264))).reshape(CB, 9 * CI)
    wc = jnp.pad(wc, ((0, 0), (0, AP - 9 * CI)))
    side = ((0, CB - CH_DEV), (0, SQP - SQ))
    sm = jnp.concatenate([jnp.pad(squeeze_weight, side), jnp.pad(excite_weight.T, side)], axis=1)
    biases = jnp.stack([first_bias, conv_bias, excite_bias], axis=1)
    fp = jnp.concatenate([jnp.pad(biases, ((0, 0), (0, 125))), second_basis], axis=1)
    fp = jnp.pad(fp, ((0, CB - CH_DEV), (0, 0)))
    fb = first_basis.reshape(GRP, CH_DEV, BASIS)
    fb = jnp.pad(fb, ((0, 0), (0, CB - CH_DEV), (0, 0))).reshape(AP, BASIS).T
    fb_top = fb.astype(bf16)
    fbt = jnp.concatenate([fb_top, (fb - fb_top.astype(f32)).astype(bf16)], axis=0)
    sqb = jnp.broadcast_to(jnp.pad(squeeze_bias, (0, SQP - SQ))[None], (8, SQP))

    V = pltpu.VMEM
    scratch = [
        V((GRP, CB, PX), bf16),
        V((GRP, CB, PX), bf16),
        V((4, CB, AP), bf16),
        V((4, CB, AP), bf16),
        V((4, CB, AP), bf16),
        V((AP, GP), bf16),
        V((AP, GP), bf16),
        V((AP, GP), bf16),
        V((4, CB, 2 * SQP), bf16),
        V((4, CB, 384), f32),
        V((4, CI, 128), bf16),
        V((4, 4, CI, 128), bf16),
        V((4, GP, 128), bf16),
        V((AP, PX), bf16),
        V((CI, PX), f32),
        V((GP, PX), f32),
        V((GP, PX), f32),
        V((GP, PX), f32),
        V((2 * BASIS, PX), bf16),
        V((2 * BASIS, GP), bf16),
        V((AP, 512), f32),
        V((2, 4, 8, CB, PX), bf16),
        V((8 * CB, PX), f32),
        V((2, 4, 8, CB, PX), bf16),
        V((2, 8, CB, PX), bf16),
        V((2, 8, CB, PX), bf16),
        V((4, CB, PX), bf16),
        V((8, 32, PX), bf16),
        V((8, 32, PX), bf16),
        V((4, 32, 640), bf16),
        V((4, 32, 640), bf16),
        V((32, 640), bf16),
        V((8, 32, 640), bf16),
        V((32, 32, 640), bf16),
        V((4, 8, 384), f32),
        V((8, 8, 384), f32),
        V((8, 8, SQP), f32),
        V((4, 8, 384), f32),
        V((8, 8, 384), f32),
        V((8, 8, SQP), f32),
        V((4, CB, PX), bf16),
        V((4, CB, PX), bf16),
        V((4, CB, BASIS), bf16),
        V((4, CB, BASIS), bf16),
        V((TILES, CB, ZC), bf16),
        V((TILES, CB, ZC), f32),
        V((TILES, CB, ZC), bf16),
        V((TILES, CB, ZC), bf16),
        pltpu.SemaphoreType.DMA((NSEM,)),
        pltpu.SemaphoreType.DMA((NSEM,)),
        pltpu.SemaphoreType.DMA((16,)),
    ]
    spec = pl.BlockSpec(memory_space=pltpu.VMEM)
    shape = jax.ShapeDtypeStruct
    bo, ig, zo, sg, se = pl.pallas_call(
        body,
        out_shape=[
            shape((4, CB, PX), bf16),
            shape((4, CB, PX), bf16),
            shape((TILES, CB, ZC), bf16),
            shape((CB, AP), f32),
            shape((4, 8, SQP), f32),
        ],
        in_specs=[spec] * 9,
        out_specs=[spec] * 5,
        scratch_shapes=scratch,
        compiler_params=pltpu.CompilerParams(
            collective_id=0, has_side_effects=True, vmem_limit_bytes=60 * 1024 * 1024
        ),
    )(xq, cq, w1, wc, w2, sm, fp, fbt, sqb)

    def pixels(v):
        v = v[:, :CH_DEV].reshape(2, 2, CH_DEV, PX).transpose(0, 1, 3, 2)
        return v.reshape(inputs.shape)

    sums = zo.transpose(1, 0, 2).reshape(CB, TILES * ZC)[:CH_DEV].astype(f32) * grad_scale
    conv_grad = sums[:, : 9 * CI].reshape(CH_DEV, 9, CI)[:, :, :264]
    first_grad = jnp.dot(first_basis, sums[:, AP : AP + BASIS].T, precision=highest)
    second_grad = (sg[:CH_DEV] * grad_scale).reshape(CH_DEV, GRP, CB)[:, :, :CH_DEV].reshape(CH_DEV, 2112)
    at = (lax.axis_index("grp") % 4) * CB
    means = lax.dynamic_slice(se[0], (0, at), (2, CH_DEV))
    sig_back = lax.dynamic_slice(se[1], (0, at), (2, CH_DEV))
    squeeze, squeeze_back = se[2, :2, :SQ], se[3, :2, :SQ]
    squeeze_grad = (means[0][:, None] * squeeze_back[0] + means[1][:, None] * squeeze_back[1]) * grad_scale
    excite_grad = (sig_back[0] * squeeze[0][:, None] + sig_back[1] * squeeze[1][:, None]) * grad_scale
    return (pixels(bo), pixels(ig), first_grad, second_grad, conv_grad, squeeze_grad, excite_grad)


def solution(mesh):
    placed = (
        P(None, "tile", None, "grp"),
        P(None, "tile", None, "grp"),
        P(None, "grp"),
        P("grp"),
        P("grp", None, None),
        P("grp"),
        P("grp", None),
        P(),
        P(None, "grp"),
        P("grp"),
        P("grp", None),
        P(),
        P("grp", None),
    )
    return jax.shard_map(
        per_device,
        mesh=mesh,
        in_specs=placed,
        out_specs=(
            P(None, "tile", None, "grp"),
            P(None, "tile", None, "grp"),
            P(None, "grp"),
            P("grp", None),
            P("grp", None, None),
            P("grp", None),
            P(None, "grp"),
        ),
        check_vma=False,
    )
```

time: 779 us -> 222 us (0.28)
  waiting for transfers between devices: 285 us -> 0 us
  blocking collectives: 280 us -> 0 us
  Pallas kernels: 0 us -> 181 us
  local copies, waits for them, and re-layouts: 91.3 us -> 30.4 us
  matrix products: 51.3 us -> 2.89 us
  starting transfers between devices: 21.9 us -> 0 us
  other arithmetic: 25.8 us -> 5.32 us
  between operations: 15.2 us -> 0.89 us
    pallas_call x0 -> x1, Pallas kernels: none -> 181 us  [per_device(): pl.pallas_call(body, out_shape=[shape((4, CB, PX), bf16), shape((4, CB, P...]
    psum x4 -> x0, blocking collectives: 143 us -> none  [the longest x1 54 us: per_device(): lax.psum(jnp.dot(means, squeeze_matrix, precision=highest), 'grp')]
    unnamed x2 -> x0, blocking collectives: 138 us -> none
    all_gather x2 -> x0, waiting for transfers between devices: 131 us -> none  [the longest x1 67.4 us: per_device(): lax.all_gather(back.reshape(images, rows_dev, col_count, ch_dev), 'grp',...]
    psum x2 -> x0, waiting for transfers between devices: 118 us -> none  [the longest x1 115 us: per_device(): lax.psum(jnp.dot(second_basis.T, second_sum, precision=highest), 'grp')]
    dot_general x19 -> x1, matrix products: 51.3 us -> 2.89 us  [per_device(): jnp.dot(first_basis, sums[:, AP:AP + BASIS].T, precision=highest)]
    unnamed x77 -> x36, local copies, waits for them, and re-layouts: 29.7 us -> 3.42 us
    ppermute x8 -> x0, waiting for transfers between devices: 23.8 us -> none  [the longest x4 21 us: swapped(): lax.ppermute(shard, axis, [(i, i ^ 1 << apart) for i in range(lax.axis_si...]
  transfers between devices with their start and end apart: 18 -> 0, of which waited for: 11 -> 0; matrix products, arithmetic and copies ran while one was open for 14% -> 0% of each run, Pallas kernels for 0% -> 0%
where the time goes in v1:
time: 222 us; the launch traced here: 220 us
  Pallas kernels  181 us (82%)
  local copies, waits for them, and re-layouts  30.4 us (14%)
  other arithmetic  5.32 us (2%)
  matrix products  2.89 us (1%)
    pallas_call x1, Pallas kernels, per_device(): pl.pallas_call(body, out_shape=[shape((4, CB, PX), bf16), shape((4, CB, P...  181 us

profile of v1, /device:TPU:2, one launch (start us, length us, event | category | flops | bytes accessed | tf_op | source)
XLA Modules:
  0.0 220.1 jit_solution(589010030853509021)
XLA Ops:
  0.6 1.7 reshape.105
  2.4 1.9 pad.55
  4.2 2.1 copy.56
  6.4 0.2 fusion
  6.6 0.0 copy-start.2
  6.6 1.7 pad_maximum_fusion.fbt
  8.3 0.4 copy.61
  8.7 0.1 pad.48.clone
  8.8 0.0 copy-start.4
  8.8 0.2 copy.54
  9.1 0.8 pad.49.wc
  9.9 1.7 reshape.100
  11.6 0.1 pad.47
  11.7 0.0 copy-start.5
  11.8 0.0 copy-start.6
  11.8 1.9 reshape.101.w1
  13.7 0.0 copy-start.11
  13.7 0.0 copy-start.9
  13.7 1.7 reshape.103
  15.5 0.1 pad.50
  15.6 1.9 reshape.104.w2
  17.5 0.2 copy.51
  17.6 0.7 pad.45
  18.3 0.2 copy.52
  18.5 0.7 pad.46
  19.2 0.1 copy.55
  19.3 0.7 pad.54.fp
  20.0 0.7 fusion.3.sm
  20.7 0.6 broadcast_in_dim.2.sqb
  21.3 180.6 %shard_map.180 = (bf16[4,80,256]{2,1,0:T(8,128)(2,1)}, bf16[4,80,256]{2,1,0:T(8,128)(2,1)}, bf16[8,80,384]{2,1,0:T(8,128)(2,1)}, f32[80,2560]{1,0:T(8,128)}, f32[4,8,640]{2,1,0:T(8,128)}) custom-call(bf16[4,80,256]{2,1,0:T(8,128)(2,1)} %bitcast.51, bf16[4,80,256]{2,1,0:T(8,128)(2,1)} %bitcast.52, bf16[80,2560]{1,0:T(8,128)(2,1)} %reshape.101.w1, ...), custom_call_target="tpu_custom_call" | custom-call | tf_op jit(solution)/shard_map/pallas_call | solution.py:598
  201.9 0.8 fusion.5
  202.6 0.1 constant_dynamic-slice_fusion
  202.7 0.8 slice_reduce_fusion.1
  203.6 0.8 add_multiply_fusion
  204.3 0.8 add_multiply_fusion.1
  205.1 1.1 convert_multiply_fusion
  206.2 0.2 copy.59
  206.4 0.1 pad.69
  206.4 0.2 copy.62
  206.6 0.9 slice.90
  207.5 3.0 %reshape.113 = f32[66,9,272]{2,1,0:T(8,128)} reshape(f32[66,2448]{1,0:T(8,128)} %slice.90) | data formatting | bytes 1292544 | tf_op jit(solution)/shard_map/reshape | solution.py:620
  210.5 2.7 %copy.60 = f32[66,9,264]{2,0,1:T(8,128)} copy(f32[66,9,264]{2,1,0:T(8,128)} %bitcast.45) | data formatting | bytes 1254528
  213.2 2.9 %convolution_bitcast_fusion = f32[2112,66]{0,1:T(8,128)} fusion(f32[2112,256]{1,0:T(8,128)S(1)} %copy-done, f32[66,3072]{1,0:T(8,128)S(1)} %bitcast.49), kind=kOutput, calls=%fused_computation | convolution fusion | flops 428212224 | bytes 2793984 | tf_op jit(solution)/shard_map/dot_general | solution.py:621
  216.1 0.1 slice_multiply_fusion
  216.2 0.6 reshape.111
  216.7 1.5 reshape.112
  218.3 0.9 copy.57
  219.2 0.9 copy.58
  (33 shorter events, 0.1 us)
Async XLA Ops:
  6.6 1.7 copy-start.2
  8.3 1.6 copy-start.3
  8.8 4.8 %copy-start.4 = (bf16[66,2112]{1,0:T(8,128)(2,1)S(1)}, bf16[66,2112]{1,0:T(8,128)(2,1)}, u32[]{:S(2)}) copy-start(bf16[66,2112]{1,0:T(8,128)(2,1)} %param.23) | copy-start | bytes 836356
  11.7 5.7 %copy-start.5 = (bf16[2,8,64,66]{3,2,1,0:T(8,128)(2,1)S(1)}, bf16[2,8,64,66]{3,2,1,0:T(8,128)(2,1)}, u32[]{:S(2)}) copy-start(bf16[2,8,64,66]{3,2,1,0:T(8,128)(2,1)} %param.13) | copy-start | bytes 405508
  11.8 6.6 %copy-start.6 = (bf16[2,8,64,66]{3,2,1,0:T(8,128)(2,1)S(1)}, bf16[2,8,64,66]{3,2,1,0:T(8,128)(2,1)}, u32[]{:S(2)}) copy-start(bf16[2,8,64,66]{3,2,1,0:T(8,128)(2,1)} %param.14) | copy-start | bytes 405508
  13.7 5.5 %copy-start.13 = (f32[66]{0:T(128)S(1)}, f32[66]{0:T(128)}, u32[]{:S(2)}) copy-start(f32[66]{0:T(128)} %param.22) | copy-start | bytes 796
  13.7 5.5 %copy-start.14 = (f32[66]{0:T(128)S(1)}, f32[66]{0:T(128)}, u32[]{:S(2)}) copy-start(f32[66]{0:T(128)} %param.18) | copy-start | bytes 796
  13.7 5.5 %copy-start.15 = (f32[66]{0:T(128)S(1)}, f32[66]{0:T(128)}, u32[]{:S(2)}) copy-start(f32[66]{0:T(128)} %param.16) | copy-start | bytes 796
  13.7 5.6 %copy-start.11 = (f32[66,256]{1,0:T(8,128)S(1)}, f32[66,256]{1,0:T(8,128)}, u32[]{:S(2)}) copy-start(f32[66,256]{1,0:T(8,128)} %param.25) | copy-start | bytes 202756
  13.7 6.3 %copy-start.9 = (bf16[528,66]{0,1:T(8,128)(2,1)S(1)}, bf16[528,66]{0,1:T(8,128)(2,1)}, u32[]{:S(2)}) copy-start(bf16[528,66]{0,1:T(8,128)(2,1)} %param.21) | copy-start | bytes 209092
  13.7 6.3 %copy-start.10 = (bf16[66,528]{1,0:T(8,128)(2,1)S(1)}, bf16[66,528]{1,0:T(8,128)(2,1)}, u32[]{:S(2)}) copy-start(bf16[66,528]{1,0:T(8,128)(2,1)} %param.19) | copy-start | bytes 209092
  15.5 5.2 %copy-start.12 = (f32[528]{0:T(1024)S(1)}, f32[528]{0:T(1024)}, u32[]{:S(2)}) copy-start(f32[528]{0:T(1024)} %param.20) | copy-start | bytes 6340
  207.5 5.7 %copy-start = (f32[2112,256]{1,0:T(8,128)S(1)}, f32[2112,256]{1,0:T(8,128)}, u32[]{:S(2)}) copy-start(f32[2112,256]{1,0:T(8,128)} %param.24) | copy-start | bytes 6488068
  210.5 5.6 %copy-start.1 = (f32[80,2560]{1,0:T(8,128)S(1)}, f32[80,2560]{1,0:T(8,128)}, u32[]{:S(2)}) copy-start(f32[80,2560]{1,0:T(8,128)} %get-tuple-element.15) | copy-start | bytes 2457604
  216.1 2.2 copy-start.8
  216.2 3.0 %copy-start.7 = (bf16[4,80,256]{2,1,0:T(8,128)(2,1)S(1)}, bf16[4,80,256]{2,1,0:T(8,128)(2,1)}, u32[]{:S(2)}) copy-start(bf16[4,80,256]{2,1,0:T(8,128)(2,1)} %get-tuple-element.13) | copy-start | bytes 491524

commit v2 on v1

v2 whole, which is shorter than its diff:
```python
import math

import jax
import jax.numpy as jnp
from jax import lax
from jax.experimental import pallas as pl
from jax.experimental.pallas import tpu as pltpu
from jax.sharding import PartitionSpec as P

MESH = pl.DeviceIdType.MESH
highest = lax.Precision.HIGHEST
bf16, f32 = jnp.bfloat16, jnp.float32

TILES = 8
GRP = 32
CH_DEV = 66
CB = 80
PX = 256
GP = 4 * CB
AP = GRP * CB
CI = 272
SQ = 528
SQP = 640
BASIS = 256
ZC = 384
CELLS = 4096.0
NSEM = 250
RAW = 2176
NCH = 2112
GRAD_SCALE = 1.0 / math.sqrt(8192.0)


def flip(index, mask):
    out = index
    for bit in range(5):
        if mask >> bit & 1:
            step = 1 << bit
            out = out + step * (1 - 2 * ((index // step) % 2))
    return out


def sigmoid(v):
    return 1.0 / (1.0 + jnp.exp(-v))


def slope(v):
    sig = sigmoid(v)
    return sig * (1.0 + v * (1.0 - sig))


def dot(a, b):
    return lax.dot_general(a, b, (((1,), (0,)), ((), ())), preferred_element_type=f32)


def dot_nt(a, b):
    return lax.dot_general(a, b, (((1,), (1,)), ((), ())), preferred_element_type=f32)


def pieces(v, count):
    out = []
    for _ in range(count - 1):
        top = v.astype(bf16)
        out.append(top)
        v = v - top.astype(f32)
    out.append(v.astype(bf16))
    return out


def dot_tn(a, b):
    return lax.dot_general(a, b, (((0,), (0,)), ((), ())), preferred_element_type=f32)


def one_hot(rows, row_start, lanes, lane_start, out_width, in_width):
    r = lax.broadcasted_iota(jnp.int32, (rows, lanes), 0) + row_start
    out = lax.broadcasted_iota(jnp.int32, (rows, lanes), 1) + lane_start
    blk = (out * ((1 << 22) // out_width + 1)) >> 22
    hit = (out - out_width * blk < CH_DEV) & (r == out + (in_width - out_width) * blk) & (blk < GRP)
    return jnp.where(hit, 1.0, 0.0).astype(bf16)


def windows(out_lanes, out_width, in_lanes, in_width):
    for start in range(0, out_lanes, 256):
        width = min(256, out_lanes - start)
        low = min(start // out_width * in_width // 128 * 128, in_lanes - 512)
        yield start, width, low


def split_left(op, a, b, count=3):
    return sum(op(p, b) for p in pieces(a, count))


def split_right(op, a, b, count=3):
    return sum(op(a, p) for p in pieces(b, count))


def body(
    xq, cq, w1, wc, w2, sqw, exw, sb_in, fb_in, side,
    bo, ig, fg, sg, cg, sqg, exg,
    xall, ball, w1p, w2p, wcp, smp, bip, w1r, w2r, w1g, wcg, w2g, smg, big,
    hots, hots2, fbp, fbn,
    ext, extg, exts, exta, cols, pre, conv_out, hidden, sback, xbt, zbuf,
    rs_far, rs_rel, rs_keep, rs_out, rs_in, rs_own, rs2_send, rs2_recv, bq,
    usend, urecv, c2s, c2r, c2z, c2zr, c2all,
    hs, hz, hb8, es, ez, eb8, hbs, hbr, c1s, c1r, zs, zf, zr, zall,
    send, recv, local,
):
    z = lax.axis_index("tile")
    me = lax.axis_index("grp")
    xx = me // 8
    col = me % 8
    m = me % 4
    g = me // 4
    core = me % 2
    img = (me // 2) % 2
    count = [0]
    started = []
    locals_ = []

    def copy(src, dst, tile, grp):
        i = count[0]
        count[0] += 1
        c = pltpu.make_async_remote_copy(
            src_ref=src, dst_ref=dst, send_sem=send.at[i], recv_sem=recv.at[i],
            device_id=(tile, grp), device_id_type=MESH,
        )
        c.start()
        started.append(c)
        return c

    def keep(src, dst):
        c = pltpu.make_async_copy(src, dst, local.at[len(locals_)])
        c.start()
        locals_.append(c)
        return c

    def peer(mask):
        return flip(me, mask)

    right, left = lax.rem(me + 8, GRP), lax.rem(me + 24, GRP)
    other = (lax.rem(z + 2 * core - 1 + TILES, TILES), flip(me, 1))
    grp_masks = [1, 2, 3, 4, 5, 6, 7, 8, 16, 24, 12, 20, 28]
    g_masks = [4, 8, 12, 16, 20, 24, 28]

    barrier = pltpu.get_barrier_semaphore()
    for mask in grp_masks:
        pl.semaphore_signal(barrier, inc=1, device_id=(z, peer(mask)), device_id_type=MESH)
    for mask in range(1, 8):
        pl.semaphore_signal(barrier, inc=1, device_id=(flip(z, mask), me), device_id_type=MESH)
    pl.semaphore_signal(barrier, inc=1, device_id=other, device_id_type=MESH)

    w1p[...] = jnp.zeros(w1p.shape, bf16)
    w1p[0:CH_DEV, 0:NCH] = w1[...]
    bip[...] = jnp.zeros(bip.shape, f32)
    bip[:, 0:8] = side[8:16, 0:128].T[0:CB]
    pl.semaphore_wait(barrier, len(grp_masks) + 8)

    def gather_column(pick, dst, slot, masks=range(1, 8)):
        return [copy(pick(k), dst.at[slot(me, 0)], z, peer(k)) for k in masks]

    def ring_start(arrived, dst, slot, masks=range(8)):
        to_right, to_left = [], []
        for n, k in enumerate(masks):
            if n:
                arrived[n - 1].wait_recv()
            at = slot(me, k)
            to_right.append(copy(dst.at[at], dst.at[at], z, right))
            to_left.append(copy(dst.at[at], dst.at[at], z, left))
        return to_right, to_left

    def ring_relay(state, dst, slot, masks=range(8)):
        to_right, to_left = state
        half = len(masks) // 2
        relayed = []
        for n in range(half):
            to_right[n].wait_recv()
            at = slot(left, masks[n])
            relayed.append(copy(dst.at[at], dst.at[at], z, right))
            to_left[n + half].wait_recv()
            at = slot(right, masks[n + half])
            relayed.append(copy(dst.at[at], dst.at[at], z, left))
        return to_right[half:] + to_left[:half] + relayed

    def group_start(src, dst):
        mine = keep(src, dst.at[m])
        return mine, copy(src, dst.at[m], z, peer(1)), copy(src, dst.at[m], z, peer(2))

    def group_forward(state, dst):
        mine, near, far = state
        far.wait_recv()
        slot = flip(m, 2)
        return mine, near, copy(dst.at[slot], dst.at[slot], z, peer(1))

    def group_finish(state):
        state[0].wait()
        state[1].wait_recv()
        state[2].wait_recv()

    def halo_start(buf):
        return (
            copy(buf.at[2 - core], buf.at[3 * core], z, peer(1)),
            copy(buf.at[1 + core], buf.at[3 - 3 * core], other[0], other[1]),
        )

    def halo_finish(buf, copies):
        for c in copies:
            c.wait_recv()

        @pl.when((z == 0) & (core == 0))
        def _():
            buf[0] = jnp.zeros(buf.shape[1:], buf.dtype)

        @pl.when((z == TILES - 1) & (core == 1))
        def _():
            buf[3] = jnp.zeros(buf.shape[1:], buf.dtype)

    def block(device, k):
        return flip(device, k)

    def bias(n):
        return big[...].reshape(GP, 128)[:, n : n + 1]

    def spread(source, target):
        for n, (start, width, low) in enumerate(windows(AP, CB, RAW, CH_DEV)):
            v = dot(source[:, :, low : low + 512].reshape(GP, 512), hots[n])
            target[:, start : start + 256] = v.astype(bf16)

    xs = gather_column(lambda k: xq.at[flip(m, k & 3)], xall, block)
    s1 = group_start(w1p, w1r)
    sbi = group_start(bip, big)
    keep(xq.at[m], xall.at[me]).wait()
    xring = ring_start(xs, xall, block)
    wcp[...] = jnp.zeros(wcp.shape, bf16)
    for t in range(9):
        wcp[0:CH_DEV, CI * t : CI * t + 264] = wc[t]
    xrows = ring_relay(xring, xall, block)
    sc = group_start(wcp, wcg)
    for n, (start, width, low) in enumerate(windows(AP, CB, RAW, CH_DEV)):
        hots[n] = one_hot(512, low, 256, start, CB, CH_DEV)
    s1 = group_forward(s1, w1r)
    sbi = group_forward(sbi, big)
    smp[...] = jnp.zeros(smp.shape, bf16)
    smp[0:CH_DEV, 0:SQ] = sqw[...]
    smp[0:CH_DEV, SQP : SQP + SQ] = exw[...]
    sb = sb_in[...]
    sb_top = sb.astype(bf16)
    smp[0:CH_DEV, 2 * SQP : 2 * SQP + BASIS] = sb_top
    smp[0:CH_DEV, 2 * SQP + BASIS :] = (sb - sb_top.astype(f32)).astype(bf16)
    w2p[...] = jnp.zeros(w2p.shape, bf16)
    w2p[0:CH_DEV, 0:NCH] = w2[...]

    def packing(shape, packed_dim):
        row = lax.broadcasted_iota(jnp.int32, shape, packed_dim)
        lane = lax.broadcasted_iota(jnp.int32, shape, 1 - packed_dim)
        shifted = row
        for part in (1, 2, 3):
            shifted = shifted + jnp.where(row >= CH_DEV * part, CB - CH_DEV, 0)
        return jnp.where((shifted == lane) & (row < 4 * CH_DEV), 1.0, 0.0).astype(bf16)

    group_finish(s1)
    spread(w1r, w1g)
    group_finish(sbi)
    for c in xrows:
        c.wait_recv()

    x_rows = xall[...].reshape(AP, PX)
    first_pre = dot(w1g[...], x_rows) + bias(0)
    active = (first_pre * sigmoid(first_pre)).astype(bf16)
    pack = packing((CI, GP), 0)
    packed = dot(pack, active).astype(bf16)
    ext[1] = packed[:, 0:128]
    ext[2] = packed[:, 128:256]
    halo = halo_start(ext)
    ssm = group_start(smp, smg)
    s2 = group_start(w2p, w2r)
    pre[...] = split_right(dot, pack, first_pre)
    sc = group_forward(sc, wcg)
    for k in range(4):
        cols[k, 9 * CI :, :] = jnp.zeros((AP - 9 * CI, PX), bf16)

    def build(read, n_target):
        lanes = lax.broadcasted_iota(jnp.int32, (16, 512), 1) % 64
        for i in range(CI // 16):
            r = 16 * i
            e = jnp.concatenate([read(n, r) for n in range(4)], axis=1).astype(f32)
            for b in (-1, 0, 1):
                if b == 0:
                    v = e
                elif b == 1:
                    v = jnp.where(lanes == 63, 0.0, pltpu.roll(e, 511, 1))
                else:
                    v = jnp.where(lanes == 0, 0.0, pltpu.roll(e, 1, 1))
                s = pltpu.roll(v, 64, 1)
                for a, win in ((-1, s[:, 128:384]), (0, v[:, 128:384]), (1, s[:, 256:512])):
                    t = 3 * (a + 1) + b + 1
                    cols[n_target, t * CI + r : t * CI + r + 16, :] = win.astype(bf16)

    halo_finish(ext, halo)
    build(lambda n, r: ext[n, r : r + 16, :], 0)
    group_finish(sc)

    co = dot(wcg[...].reshape(GP, AP), cols[0]) + bias(1)
    conv_out[...] = co
    hid = co * sigmoid(co)
    hidden[...] = hid
    ones = jnp.ones((8, PX), bf16)
    rows8 = lax.broadcasted_iota(jnp.int32, (8, 128), 0)

    def sums_start(v, buf):
        tile = jnp.zeros((8, 128), f32)
        for j in range(3):
            part = v[128 * j : min(128 * (j + 1), GP)]
            if j == 2:
                part = jnp.concatenate([part, jnp.zeros((64, PX), f32)], axis=0)
            tile = jnp.where(rows8 == 3 * img + j, split_right(dot_nt, ones, part), tile)
        buf[0] = tile
        return [copy(buf.at[0], buf.at[k], z, peer(k)) for k in range(1, 4)]

    def sums_tiles(copies, buf, wider):
        for c in copies:
            c.wait_recv()
        wider[0] = buf[0] + buf[1] + buf[2] + buf[3]
        return [copy(wider.at[0], wider.at[k], flip(z, k), me) for k in (4, 3, 5, 2, 6, 1, 7)]

    def sums_finish(copies, wider):
        for c in copies:
            c.wait_recv()
        tile = sum(wider[k] for k in range(8))
        parts = [
            jnp.where(rows8 == 0, tile[j : j + 1], jnp.where(rows8 == 1, tile[3 + j : 4 + j], 0.0))
            for j in range(3)
        ]
        return jnp.concatenate(parts, axis=1)[:, 0:GP]

    def squeeze_start(v, buf):
        low, high = jnp.zeros((8, 128), f32), jnp.zeros((8, 128), f32)
        for j in range(5):
            part = v[:, 128 * j : 128 * (j + 1)]
            low = jnp.where(rows8 == j, part[0:1], low)
            high = jnp.where(rows8 == j, part[1:2], high)
        buf[0, 0] = low
        buf[0, 1] = high
        return [copy(buf.at[0], buf.at[n + 1], z, peer(k)) for n, k in enumerate(g_masks)]

    def squeeze_finish(copies, buf):
        for c in copies:
            c.wait_recv()
        low = sum(buf[n, 0] for n in range(8))
        high = sum(buf[n, 1] for n in range(8))
        parts = [
            jnp.where(rows8 == 0, low[j : j + 1], jnp.where(rows8 == 1, high[j : j + 1], 0.0))
            for j in range(5)
        ]
        return jnp.concatenate(parts, axis=1)

    ah = sums_start(hid, hs)
    ssm = group_forward(ssm, smg)
    sext = group_start(ext, extg)
    sh = sums_tiles(ah, hs, hz)
    s2 = group_forward(s2, w2r)
    group_finish(ssm)
    means = sums_finish(sh, hz) * (1.0 / CELLS)
    sq_w = smg[:, :, 0:SQP].reshape(GP, SQP)
    ex_w = smg[:, :, SQP : 2 * SQP].reshape(GP, SQP)
    bh = squeeze_start(split_left(dot, means, sq_w), hb8)
    group_finish(s2)
    spread(w2r, w2g)
    squeeze_pre = squeeze_finish(bh, hb8) + side[0:8]
    squeeze = squeeze_pre * sigmoid(squeeze_pre)
    excite = sigmoid(split_right(dot_nt, ex_w, squeeze) + bias(2))
    ex_col = jnp.where(img == 0, excite[:, 0:1], excite[:, 1:2])
    scaled = (hidden[...] * ex_col).astype(bf16)

    def reduce_start(weights, rhs, inner):
        def part(step):
            at = pl.multiple_of(lax.rem(xx + step, 4) * (8 * CB), 128)
            return dot_tn(weights[:, pl.ds(at, 8 * CB)], rhs).reshape(8, CB, PX)

        rs_far[inner] = part(2).astype(bf16)
        far = [
            copy(rs_far.at[inner, 0:4], rs_rel.at[inner, 0], z, right),
            copy(rs_far.at[inner, 4:8], rs_rel.at[inner, 1], z, left),
        ]
        p = part(1)
        rs_out[inner, 0, 4:8] = p[4:8].astype(bf16)
        near = [copy(rs_out.at[inner, 0, 4:8], rs_in.at[inner, 0, 4:8], z, right)]
        rs_keep[0] = p[0:4]
        p = part(3)
        rs_out[inner, 1, 0:4] = p[0:4].astype(bf16)
        near.append(copy(rs_out.at[inner, 1, 0:4], rs_in.at[inner, 1, 0:4], z, left))
        rs_keep[1] = p[4:8]
        rs_own[...] = part(0)
        return far, near

    def reduce_relay(state, inner):
        far, near = state
        far[0].wait_recv()
        rs_out[inner, 0, 0:4] = (rs_keep[0] + rs_rel[inner, 0].astype(f32)).astype(bf16)
        near.append(copy(rs_out.at[inner, 0, 0:4], rs_in.at[inner, 0, 0:4], z, right))
        far[1].wait_recv()
        rs_out[inner, 1, 4:8] = (rs_keep[1] + rs_rel[inner, 1].astype(f32)).astype(bf16)
        near.append(copy(rs_out.at[inner, 1, 4:8], rs_in.at[inner, 1, 4:8], z, left))
        return near

    def reduce_column(copies, inner):
        for c in copies:
            c.wait_recv()
        total = rs_own[...] + rs_in[inner, 0].astype(f32) + rs_in[inner, 1].astype(f32)
        rs2_send[inner] = total.astype(bf16)
        return [
            copy(rs2_send.at[inner, flip(col, k)], rs2_recv.at[inner, k], z, peer(k))
            for k in range(1, 8)
        ]

    def reduce_quarter(copies, inner, kk):
        copies[kk + 3].wait_recv()
        if kk:
            copies[kk - 1].wait_recv()
            first = rs2_recv[inner, kk]
        else:
            first = rs2_send[inner, col]
        return first.astype(f32) + rs2_recv[inner, kk + 4].astype(f32)

    r1 = reduce_start(w2g, scaled, 0)
    sl = slope(conv_out[...]).astype(bf16)
    for n in range(2):
        exts[n + 1] = sl[:, 128 * n : 128 * (n + 1)]
    halo_s = halo_start(exts)
    sext = group_forward(sext, extg)
    sb_top = smg[:, :, 2 * SQP : 2 * SQP + BASIS].reshape(GP, BASIS)
    sb_low = smg[:, :, 2 * SQP + BASIS :].reshape(GP, BASIS)
    u2 = dot_tn(sb_top, scaled) + dot_tn(sb_low, scaled)
    usend[...] = u2.astype(bf16).reshape(8, 32, PX)
    us = [copy(usend.at[flip(g, k // 4)], urecv.at[n + 1], z, peer(k)) for n, k in enumerate(g_masks)]
    r1 = reduce_relay(r1, 0)
    for b in range(GRP):
        v = fb_in[CH_DEV * b : CH_DEV * (b + 1), :]
        v = jnp.concatenate([v, jnp.zeros((CB - CH_DEV, BASIS), f32)], axis=0)
        top = v.astype(bf16)
        fbp[0, CB * b : CB * (b + 1), :] = top
        fbp[1, CB * b : CB * (b + 1), :] = (v - top.astype(f32)).astype(bf16)
    xb = dot_tn(fbp[0], x_rows) + dot_tn(fbp[1], x_rows)
    xb_top = xb.astype(bf16)
    xbt[0:BASIS, :] = xb_top
    xbt[BASIS:, :] = (xb - xb_top.astype(f32)).astype(bf16)
    ex_row = sigmoid(
        split_left(dot_nt, squeeze, ex_w)
        + split_right(
            dot_nt,
            jnp.where(lax.broadcasted_iota(jnp.int32, (8, 128), 1) == 2, 1.0, 0.0).astype(bf16),
            big[...].reshape(GP, 128),
        )
    )
    halo_finish(exts, halo_s)
    c2cols = reduce_column(r1, 0)
    back_copies = [None] * 7
    for kk in range(4):
        q = flip(m, kk)
        total = xq[q].astype(f32) + reduce_quarter(c2cols, 0, kk)
        sig = sigmoid(total)
        bo[q] = (total * sig).astype(bf16)
        bq[q] = (cq[q].astype(f32) * (sig * (1.0 + total * (1.0 - sig)))).astype(bf16)
        for k in (kk, kk + 4):
            if k:
                back_copies[k - 1] = copy(bq.at[q], ball.at[me], z, peer(k))
    ball[me] = bq[m]
    bring = ring_start(back_copies, ball, block)
    brows = ring_relay(bring, ball, block)
    for c in us:
        c.wait_recv()
    u_own = usend[g].astype(f32)
    for n in range(1, 8):
        u_own = u_own + urecv[n].astype(f32)
    u_top = u_own.astype(bf16)
    u_low = (u_own - u_top.astype(f32)).astype(bf16)
    group_finish(sext)

    def build_other(k, carry):
        q = m + (k % 2) * (1 - 2 * (m % 2)) + 2 * (k // 2) * (1 - 2 * (m // 2))
        build(lambda n, r: extg[q, n, r : r + 16, :], k)
        return carry

    lax.fori_loop(1, 4, build_other, 0)
    for c in brows:
        c.wait_recv()

    back_rows = ball[...].reshape(AP, PX)
    scaled_back = dot(w2g[...], back_rows)
    ae = sums_start(scaled_back * hidden[...], es)
    scaled_back = scaled_back * ex_col
    sback[...] = scaled_back
    edge = scaled_back.astype(bf16)
    for n in range(2):
        exta[n + 1] = edge[:, 128 * n : 128 * (n + 1)]
    halo_a = halo_start(exta)
    se_ = sums_tiles(ae, es, ez)
    coords = dot_nt(u_top, back_rows) + dot_nt(u_low, back_rows)
    for k in range(4):
        c2s[k] = coords[:, 640 * k : 640 * (k + 1)].astype(bf16)
    c2g = [copy(c2s.at[flip(m, k)], c2r.at[k], z, peer(k)) for k in range(1, 4)]
    excite_back = sums_finish(se_, ez)
    sig_back = excite_back * ex_row * (1.0 - ex_row)
    be = squeeze_start(split_left(dot, sig_back, ex_w), eb8)
    halo_finish(exta, halo_a)
    squeeze_back = squeeze_finish(be, eb8) * slope(squeeze_pre)
    means_back = split_right(dot_nt, sq_w, squeeze_back)
    mb_col = jnp.where(img == 0, means_back[:, 0:1], means_back[:, 1:2]) * (1.0 / CELLS)
    hb = ((sback[...] + mb_col) * slope(conv_out[...])).astype(bf16)
    hbs[...] = hb.reshape(4, CB, PX)
    hsw = [copy(hbs.at[flip(m, k)], hbr.at[k], z, peer(k)) for k in range(1, 4)]
    before, after = [
        ((exta[n].astype(f32) + mb_col) * exts[n].astype(f32)).astype(bf16) for n in (0, 3)
    ]
    hb_wide = jnp.concatenate([before, hb, after], axis=1)

    zbuf[...] = dot_tn(wcg[...].reshape(GP, AP), hb_wide)
    lanes8 = lax.broadcasted_iota(jnp.int32, (16, PX), 1) % 64
    for i in range(CI // 16):
        r = 16 * i
        acc = jnp.zeros((16, PX), f32)
        for b in (-1, 0, 1):
            up = zbuf[CI * (b + 1) + r : CI * (b + 1) + r + 16, :]
            mid = zbuf[CI * (b + 4) + r : CI * (b + 4) + r + 16, :]
            down = zbuf[CI * (b + 7) + r : CI * (b + 7) + r + 16, :]
            y = mid[:, 128:384] + pltpu.roll(up, 64, 1)[:, 256:512] + pltpu.roll(down, 64, 1)[:, 128:384]
            if b == 1:
                y = jnp.where(lanes8 == 0, 0.0, pltpu.roll(y, 1, 1))
            elif b == -1:
                y = jnp.where(lanes8 == 63, 0.0, pltpu.roll(y, PX - 1, 1))
            acc = acc + y
        pre[r : r + 16, :] = acc * slope(pre[r : r + 16, :])
    unpack = packing((GP, CI), 1)
    ag = dot(unpack, pre[...].astype(bf16)).astype(bf16)
    r2 = reduce_start(w1g, ag, 1)

    c1 = dot_nt(ag, xbt[0:BASIS, :]) + dot_nt(ag, xbt[BASIS:, :])
    c1s[...] = c1.astype(bf16).reshape(4, CB, BASIS)
    c1g = [copy(c1s.at[flip(m, k)], c1r.at[k], z, peer(k)) for k in range(1, 4)]
    for c in c2g:
        c.wait_recv()
    c2 = c2s[m].astype(f32) + c2r[1].astype(f32) + c2r[2].astype(f32) + c2r[3].astype(f32)
    c2z[...] = c2.astype(bf16)
    c2t = [copy(c2z, c2zr.at[k], flip(z, k), me) for k in range(1, 8)]
    r2 = reduce_relay(r2, 1)
    for c in hsw:
        c.wait_recv()
    grads = dot_nt(hbs[m], cols[0])
    for k in range(1, 4):
        grads = grads + dot_nt(hbr[k], cols[k])
    for c in c1g:
        c.wait_recv()
    c1 = c1s[m].astype(f32) + c1r[1].astype(f32) + c1r[2].astype(f32) + c1r[3].astype(f32)
    both = jnp.concatenate([grads, c1, jnp.zeros((CB, TILES * ZC - AP - BASIS), f32)], axis=1)
    for k in range(TILES):
        zf[k] = both[:, ZC * k : ZC * (k + 1)]
        zs[k] = both[:, ZC * k : ZC * (k + 1)].astype(bf16)
    z1 = [copy(zs.at[flip(z, k)], zr.at[k], flip(z, k), me) for k in range(1, 8)]
    for c in c2t:
        c.wait_recv()
    c2 = c2z[...].astype(f32)
    for k in range(1, 8):
        c2 = c2 + c2zr[k].astype(f32)

    def slot2(device, k):
        d = flip(device, k)
        return (d % 4) * 8 + d // 4

    same = (0, 2, 4, 6)
    c2all[slot2(me, 0)] = c2.astype(bf16)
    c2c = gather_column(lambda k: c2all.at[slot2(me, 0)], c2all, slot2, same[1:])
    c2cols = reduce_column(r2, 1)
    c2ring = ring_start(c2c, c2all, slot2, same)
    for c in z1:
        c.wait_recv()
    chunk = zf[z]
    for k in range(1, 8):
        chunk = chunk + zr[k].astype(f32)
    zall[z] = chunk.astype(bf16)
    z2 = [copy(zall.at[z], zall.at[z], flip(z, k), me) for k in range(1, 8)]
    c2rows = ring_relay(c2ring, c2all, slot2, same)
    for kk in range(4):
        q = flip(m, kk)
        ig[q] = (bq[q].astype(f32) + reduce_quarter(c2cols, 1, kk)).astype(bf16)
    swaps = [copy(c2all.at[slot2(me, k)], c2all.at[slot2(me, k)], z, peer(1)) for k in same]
    for c in c2rows:
        c.wait_recv()
    for step in (1, 2, 3):
        there = lax.rem(me + 8 * step, GRP)
        for k in same:
            at = slot2(there, k)
            swaps.append(copy(c2all.at[at], c2all.at[at], z, peer(1)))

    first = lax.broadcasted_iota(jnp.int32, (CB, GP), 0) + CB * m
    mine = jnp.where(first == lax.broadcasted_iota(jnp.int32, (CB, GP), 1), 1.0, 0.0).astype(bf16)
    own = split_right(dot_nt, mine, means)
    grad = own[:, 0:1] * squeeze_back[0:1] + own[:, 1:2] * squeeze_back[1:2]
    sqg[...] = (grad * GRAD_SCALE)[0:CH_DEV, 0:SQ]
    own = split_right(dot_nt, mine, sig_back)
    grad = own[:, 0:1] * squeeze[0:1] + own[:, 1:2] * squeeze[1:2]
    exg[...] = (grad * GRAD_SCALE)[0:CH_DEV, 0:SQ]
    for n, (start, width, low) in enumerate(windows(NCH, CH_DEV, AP, CB)):
        hots2[n] = one_hot(512, low, 256, start, CH_DEV, CB)
    fb = fb_in[...]
    top = fb.astype(bf16)
    fbn[0] = top
    fbn[1] = (fb - top.astype(f32)).astype(bf16)
    for c in swaps:
        c.wait_recv()
    wide = jnp.concatenate([c2all[8 * k : 8 * (k + 1)].reshape(BASIS, 640) for k in range(4)], axis=1)
    own_top = smp[:, 2 * SQP : 2 * SQP + BASIS]
    own_low = smp[:, 2 * SQP + BASIS :]
    for n, (start, width, low) in enumerate(windows(NCH, CH_DEV, AP, CB)):
        v = dot(wide[:, low : low + 512], hots2[n]).astype(bf16)
        v = (dot(own_top, v) + dot(own_low, v)) * GRAD_SCALE
        sg[:, start : start + width] = v[0:CH_DEV, 0:width]
    for c in z2:
        c.wait_recv()
    lanes_left = AP - ZC * 6
    c1 = jnp.concatenate([zall[6, :, lanes_left:], zall[7, :, 0 : BASIS - (ZC - lanes_left)]], axis=1)
    v = (dot_nt(c1, fbn[0]) + dot_nt(c1, fbn[1])) * GRAD_SCALE
    fg[...] = v[0:CH_DEV]
    sums = jnp.concatenate([zall[k] for k in range(7)], axis=1).astype(f32) * GRAD_SCALE
    for t in range(9):
        cg[t] = sums[0:CH_DEV, CI * t : CI * t + 264]
    for c in started:
        c.wait_send()


def per_device(
    inputs,
    cotangent,
    first_weight,
    first_bias,
    conv_weight,
    conv_bias,
    squeeze_weight,
    squeeze_bias,
    excite_weight,
    excite_bias,
    second_weight,
    first_basis,
    second_basis,
):
    def quarters(v):
        v = v.reshape(2, 2, PX, CH_DEV).transpose(0, 1, 3, 2)
        return jnp.pad(v, ((0, 0), (0, 0), (0, CB - CH_DEV), (0, 0))).reshape(4, CB, PX)

    xq, cq = quarters(inputs), quarters(cotangent)
    biases = jnp.pad(jnp.stack([first_bias, conv_bias, excite_bias]), ((0, 5), (0, SQP - CH_DEV)))
    squeeze_rows = jnp.broadcast_to(jnp.pad(squeeze_bias, (0, SQP - SQ))[None], (8, SQP))
    side = jnp.concatenate([squeeze_rows, biases])

    V = pltpu.VMEM
    scratch = [
        V((GRP, CB, PX), bf16),
        V((GRP, CB, PX), bf16),
        V((CB, RAW), bf16),
        V((CB, RAW), bf16),
        V((CB, AP), bf16),
        V((CB, 2 * SQP + 2 * BASIS), bf16),
        V((CB, 128), f32),
        V((4, CB, RAW), bf16),
        V((4, CB, RAW), bf16),
        V((GP, AP), bf16),
        V((4, CB, AP), bf16),
        V((GP, AP), bf16),
        V((4, CB, 2 * SQP + 2 * BASIS), bf16),
        V((4, CB, 128), f32),
        V((10, 512, 256), bf16),
        V((9, 512, 256), bf16),
        V((2, AP, BASIS), bf16),
        V((2, NCH, BASIS), bf16),
        V((4, CI, 128), bf16),
        V((4, 4, CI, 128), bf16),
        V((4, GP, 128), bf16),
        V((4, GP, 128), bf16),
        V((4, AP, PX), bf16),
        V((CI, PX), f32),
        V((GP, PX), f32),
        V((GP, PX), f32),
        V((GP, PX), f32),
        V((2 * BASIS, PX), bf16),
        V((AP, 512), f32),
        V((2, 8, CB, PX), bf16),
        V((2, 2, 4, CB, PX), bf16),
        V((2, 4, CB, PX), f32),
        V((2, 2, 8, CB, PX), bf16),
        V((2, 2, 8, CB, PX), bf16),
        V((8, CB, PX), f32),
        V((2, 8, CB, PX), bf16),
        V((2, 8, CB, PX), bf16),
        V((4, CB, PX), bf16),
        V((8, 32, PX), bf16),
        V((8, 32, PX), bf16),
        V((4, 32, 640), bf16),
        V((4, 32, 640), bf16),
        V((32, 640), bf16),
        V((8, 32, 640), bf16),
        V((32, 32, 640), bf16),
        V((4, 8, 128), f32),
        V((8, 8, 128), f32),
        V((8, 2, 8, 128), f32),
        V((4, 8, 128), f32),
        V((8, 8, 128), f32),
        V((8, 2, 8, 128), f32),
        V((4, CB, PX), bf16),
        V((4, CB, PX), bf16),
        V((4, CB, BASIS), bf16),
        V((4, CB, BASIS), bf16),
        V((TILES, CB, ZC), bf16),
        V((TILES, CB, ZC), f32),
        V((TILES, CB, ZC), bf16),
        V((TILES, CB, ZC), bf16),
        pltpu.SemaphoreType.DMA((NSEM,)),
        pltpu.SemaphoreType.DMA((NSEM,)),
        pltpu.SemaphoreType.DMA((16,)),
    ]
    spec = pl.BlockSpec(memory_space=pltpu.VMEM)
    shape = jax.ShapeDtypeStruct
    bo, ig, fg, sg, cg, sqg, exg = pl.pallas_call(
        body,
        out_shape=[
            shape((4, CB, PX), bf16),
            shape((4, CB, PX), bf16),
            shape((CH_DEV, NCH), f32),
            shape((CH_DEV, NCH), f32),
            shape((9, CH_DEV, 264), f32),
            shape((CH_DEV, SQ), f32),
            shape((CH_DEV, SQ), f32),
        ],
        in_specs=[spec] * 10,
        out_specs=[spec] * 7,
        scratch_shapes=scratch,
        compiler_params=pltpu.CompilerParams(
            collective_id=0, has_side_effects=True, vmem_limit_bytes=62 * 1024 * 1024
        ),
    )(
        xq, cq, first_weight.T, conv_weight.transpose(1, 0, 2), second_weight,
        squeeze_weight, excite_weight.T, second_basis, first_basis, side,
    )

    def pixels(v):
        v = v[:, :CH_DEV].reshape(2, 2, CH_DEV, PX).transpose(0, 1, 3, 2)
        return v.reshape(inputs.shape)

    return (pixels(bo), pixels(ig), fg.T, sg, cg.transpose(1, 0, 2), sqg, exg.T)


def solution(mesh):
    placed = (
        P(None, "tile", None, "grp"),
        P(None, "tile", None, "grp"),
        P(None, "grp"),
        P("grp"),
        P("grp", None, None),
        P("grp"),
        P("grp", None),
        P(),
        P(None, "grp"),
        P("grp"),
        P("grp", None),
        P(),
        P("grp", None),
    )
    return jax.shard_map(
        per_device,
        mesh=mesh,
        in_specs=placed,
        out_specs=(
            P(None, "tile", None, "grp"),
            P(None, "tile", None, "grp"),
            P(None, "grp"),
            P("grp", None),
            P("grp", None, None),
            P("grp", None),
            P(None, "grp"),
        ),
        check_vma=False,
    )
```

time: 222 us -> 171 us (0.77)
  Pallas kernels: 181 us -> 156 us
  local copies, waits for them, and re-layouts: 30.4 us -> 13.1 us
  other arithmetic: 5.32 us -> 1.32 us
  matrix products: 2.89 us -> 0 us
    pallas_call x1, Pallas kernels: 181 us -> 156 us  [per_device(): pl.pallas_call(body, out_shape=[shape((4, CB, PX), bf16), shape((4, CB, P...]
    reshape x10 -> x0, local copies, waits for them, and re-layouts: 16.4 us -> none  [the longest x2 3.77 us: spread(): jnp.pad(v, ((0, CB - CH_DEV), (0, 0), (0, CB - CH_DEV))).reshape(CB, AP)]
    pad x7 -> x1, local copies, waits for them, and re-layouts: 3.66 us -> 0.69 us  [per_device(): jnp.pad(squeeze_bias, (0, SQP - SQ))[None]]
    dot_general x1 -> x0, matrix products: 2.89 us -> none  [per_device(): jnp.dot(first_basis, sums[:, AP:AP + BASIS].T, precision=highest)]
    mul x4 -> x0, other arithmetic: 2.7 us -> none  [the longest x1 1.09 us: per_device(): zo.transpose(1, 0, 2).reshape(CB, TILES * ZC)[:CH_DEV].astype(f32)]
    slice x3 -> x0, local copies, waits for them, and re-layouts: 2.51 us -> none  [the longest x1 0.92 us: per_device(): conv_grad = sums[:, :9 * CI].reshape(CH_DEV, 9, CI)[:, :, :264]]
    unnamed x36 -> x13, local copies, waits for them, and re-layouts: 3.42 us -> 5.13 us
where the time goes in v2:
time: 171 us
  Pallas kernels  156 us (91%)
  local copies, waits for them, and re-layouts  13.1 us (8%)
    pallas_call x1, Pallas kernels, per_device(): pl.pallas_call(body, out_shape=[shape((4, CB, PX), bf16), shape((4, CB, P...  156 us
    unnamed x13, local copies, waits for them, and re-layouts  5.13 us

profile of v2, /device:TPU:2, one launch (start us, length us, event | category | flops | bytes accessed | tf_op | source)
XLA Modules:
  0.0 170.7 jit_solution(12322285513957770310)
XLA Ops:
  0.6 1.1 copy.20
  1.7 0.7 pad.15
  2.4 1.1 copy.21
  3.5 0.7 pad.16
  4.2 0.7 pad.17
  4.9 0.7 select_maximum_fusion
  5.6 0.6 pad_maximum_fusion.side
  6.2 155.6 %shard_map.180 = (bf16[4,80,256]{2,1,0:T(8,128)(2,1)}, bf16[4,80,256]{2,1,0:T(8,128)(2,1)}, f32[66,2112]{1,0:T(8,128)}, f32[66,2112]{1,0:T(8,128)}, f32[9,66,264...) custom-call(bf16[4,80,256]{2,1,0:T(8,128)(2,1)} %bitcast.24, bf16[4,80,256]{2,1,0:T(8,128)(2,1)} %bitcast.25, ...), custom_call_target="tpu_custom_call" | custom-call | tf_op jit(solution)/shard_map/pallas_call | solution.py:719
  161.9 0.0 copy-start.1
  161.9 0.0 copy-start
  161.9 1.0 slice.6
  162.9 0.9 copy.22
  163.8 0.9 slice.7
  164.7 0.9 copy.23
  165.6 0.0 copy-start.3
  165.6 0.0 copy-start.2
  165.6 2.0 %copy.29 = f32[2112,66]{0,1:T(8,128)} copy(f32[2112,66]{0,1:T(8,128)} %bitcast.26) | data formatting | bytes 1115136
  167.6 0.0 copy-done.1
  167.6 0.8 copy.30
  168.4 0.0 copy-done
  168.4 0.9 copy.31
  169.3 0.0 copy-done.3
  169.4 0.7 copy.32
  170.0 0.0 copy-done.2
  170.0 0.7 copy.33
  (1 shorter events, 0.0 us)
Async XLA Ops:
  161.9 5.7 %copy-start.1 = (f32[66,2112]{1,0:T(8,128)S(1)}, f32[66,2112]{1,0:T(8,128)}, u32[]{:S(2)}) copy-start(f32[66,2112]{1,0:T(8,128)} %get-tuple-element.31) | copy-start | bytes 1672708
  161.9 6.5 %copy-start = (f32[9,66,264]{2,1,0:T(8,128)S(1)}, f32[9,66,264]{2,1,0:T(8,128)}, u32[]{:S(2)}) copy-start(f32[9,66,264]{2,1,0:T(8,128)} %get-tuple-element.18) | copy-start | bytes 1881796
  165.6 3.8 %copy-start.3 = (f32[66,528]{1,0:T(8,128)S(1)}, f32[66,528]{1,0:T(8,128)}, u32[]{:S(2)}) copy-start(f32[66,528]{1,0:T(8,128)} %get-tuple-element.33) | copy-start | bytes 418180
  165.6 4.5 %copy-start.2 = (f32[66,528]{1,0:T(8,128)S(1)}, f32[66,528]{1,0:T(8,128)}, u32[]{:S(2)}) copy-start(f32[66,528]{1,0:T(8,128)} %get-tuple-element.20) | copy-start | bytes 418180

commit v3 on v2

--- a/solution.py
+++ b/solution.py
@@ -94,12 +94,12 @@
 
 
 def body(
-    xq, cq, w1, wc, w2, sqw, exw, sb_in, fb_in, side,
-    bo, ig, fg, sg, cg, sqg, exg,
-    xall, ball, w1p, w2p, wcp, smp, bip, w1r, w2r, w1g, wcg, w2g, smg, big,
+    x_in, c_in, w1, wc, w2, sqw, exw, sb_in, fb_hbm, b1, b2, b3, b4,
+    bo_out, ig_out, fg, sg, cg, sqg, exg,
+    xq, cq, fb_in, bt, sqb, xall, ball, w1p, w2p, wcp, smp, bip, w1r, w2r, w1g, wcg, w2g, smg, big,
     hots, hots2, fbp, fbn,
     ext, extg, exts, exta, cols, pre, conv_out, hidden, sback, xbt, zbuf,
-    rs_far, rs_rel, rs_keep, rs_out, rs_in, rs_own, rs2_send, rs2_recv, bq,
+    bo, rs_far, rs_rel, rs_keep, rs_out, rs_in, rs_own, rs2_send, rs2_recv, bq,
     usend, urecv, c2s, c2r, c2z, c2zr, c2all,
     hs, hz, hb8, es, ez, eb8, hbs, hbr, c1s, c1r, zs, zf, zr, zall,
     send, recv, local,
@@ -148,10 +148,18 @@
         pl.semaphore_signal(barrier, inc=1, device_id=(flip(z, mask), me), device_id_type=MESH)
     pl.semaphore_signal(barrier, inc=1, device_id=other, device_id_type=MESH)
 
+    fb_copy = keep(fb_hbm, fb_in)
+    diagonal = lax.broadcasted_iota(jnp.int32, (CB, CH_DEV), 0) == lax.broadcasted_iota(jnp.int32, (CB, CH_DEV), 1)
+    eye = jnp.where(diagonal, 1.0, 0.0).astype(bf16)
+    for q in range(4):
+        xq[q] = dot_nt(eye, x_in[q]).astype(bf16)
     w1p[...] = jnp.zeros(w1p.shape, bf16)
     w1p[0:CH_DEV, 0:NCH] = w1[...]
+    bt[...] = jnp.zeros(bt.shape, f32)
+    for n, vector in enumerate((b1, b2, b3)):
+        bt[n : n + 1, 0:CH_DEV] = vector[...]
     bip[...] = jnp.zeros(bip.shape, f32)
-    bip[:, 0:8] = side[8:16, 0:128].T[0:CB]
+    bip[:, 0:8] = bt[...].T[0:CB]
     pl.semaphore_wait(barrier, len(grp_masks) + 8)
 
     def gather_column(pick, dst, slot, masks=range(1, 8)):
@@ -229,6 +237,8 @@
     sbi = group_start(bip, big)
     keep(xq.at[m], xall.at[me]).wait()
     xring = ring_start(xs, xall, block)
+    sqb[...] = jnp.zeros(sqb.shape, f32)
+    sqb[0:1, 0:SQ] = b4[...]
     wcp[...] = jnp.zeros(wcp.shape, bf16)
     for t in range(9):
         wcp[0:CH_DEV, CI * t : CI * t + 264] = wc[t]
@@ -247,6 +257,8 @@
     smp[0:CH_DEV, 2 * SQP + BASIS :] = (sb - sb_top.astype(f32)).astype(bf16)
     w2p[...] = jnp.zeros(w2p.shape, bf16)
     w2p[0:CH_DEV, 0:NCH] = w2[...]
+    for q in range(4):
+        cq[q] = dot_nt(eye, c_in[q]).astype(bf16)
 
     def packing(shape, packed_dim):
         row = lax.broadcasted_iota(jnp.int32, shape, packed_dim)
@@ -358,58 +370,87 @@
     sh = sums_tiles(ah, hs, hz)
     s2 = group_forward(s2, w2r)
     group_finish(ssm)
+    fb_copy.wait()
+    for b in range(GRP):
+        v = fb_in[CH_DEV * b : CH_DEV * (b + 1), :]
+        v = jnp.concatenate([v, jnp.zeros((CB - CH_DEV, BASIS), f32)], axis=0)
+        top = v.astype(bf16)
+        fbp[0, CB * b : CB * (b + 1), :] = top
+        fbp[1, CB * b : CB * (b + 1), :] = (v - top.astype(f32)).astype(bf16)
     means = sums_finish(sh, hz) * (1.0 / CELLS)
     sq_w = smg[:, :, 0:SQP].reshape(GP, SQP)
     ex_w = smg[:, :, SQP : 2 * SQP].reshape(GP, SQP)
     bh = squeeze_start(split_left(dot, means, sq_w), hb8)
     group_finish(s2)
     spread(w2r, w2g)
-    squeeze_pre = squeeze_finish(bh, hb8) + side[0:8]
+    xb = dot_tn(fbp[0], x_rows) + dot_tn(fbp[1], x_rows)
+    xb_top = xb.astype(bf16)
+    xbt[0:BASIS, :] = xb_top
+    xbt[BASIS:, :] = (xb - xb_top.astype(f32)).astype(bf16)
+    squeeze_pre = squeeze_finish(bh, hb8) + sqb[0:1]
     squeeze = squeeze_pre * sigmoid(squeeze_pre)
     excite = sigmoid(split_right(dot_nt, ex_w, squeeze) + bias(2))
     ex_col = jnp.where(img == 0, excite[:, 0:1], excite[:, 1:2])
     scaled = (hidden[...] * ex_col).astype(bf16)
 
+    unit_a, unit_b, unit_c, unit_d = 2, 3, 1, 0
+
+    def unit(r):
+        return pl.ds(2 * flip(col // 2, r), 2)
+
+    def reduce_send(inner, side, r, device):
+        at = unit(r)
+        return copy(rs_out.at[inner, side, at], rs_in.at[inner, side, at], z, device)
+
+    def reduce_near(inner, side, r, device):
+        at = unit(r)
+        rs_out[inner, side, at] = rs_keep[side, at].astype(bf16)
+        return reduce_send(inner, side, r, device)
+
+    def reduce_pass(inner, side, r, device, arrived):
+        at = unit(r)
+        arrived.wait_recv()
+        rs_out[inner, side, at] = (rs_keep[side, at] + rs_rel[inner, at].astype(f32)).astype(bf16)
+        return reduce_send(inner, side, r, device)
+
     def reduce_start(weights, rhs, inner):
         def part(step):
             at = pl.multiple_of(lax.rem(xx + step, 4) * (8 * CB), 128)
             return dot_tn(weights[:, pl.ds(at, 8 * CB)], rhs).reshape(8, CB, PX)
 
         rs_far[inner] = part(2).astype(bf16)
-        far = [
-            copy(rs_far.at[inner, 0:4], rs_rel.at[inner, 0], z, right),
-            copy(rs_far.at[inner, 4:8], rs_rel.at[inner, 1], z, left),
-        ]
-        p = part(1)
-        rs_out[inner, 0, 4:8] = p[4:8].astype(bf16)
-        near = [copy(rs_out.at[inner, 0, 4:8], rs_in.at[inner, 0, 4:8], z, right)]
-        rs_keep[0] = p[0:4]
-        p = part(3)
-        rs_out[inner, 1, 0:4] = p[0:4].astype(bf16)
-        near.append(copy(rs_out.at[inner, 1, 0:4], rs_in.at[inner, 1, 0:4], z, left))
-        rs_keep[1] = p[4:8]
+        far = {}
+        for r, device in ((unit_a, right), (unit_c, left), (unit_b, right), (unit_d, left)):
+            far[r] = copy(rs_far.at[inner, unit(r)], rs_rel.at[inner, unit(r)], z, device)
+        rs_keep[0] = part(1)
+        near = {(0, unit_c): reduce_near(inner, 0, unit_c, right)}
+        rs_keep[1] = part(3)
+        near[1, unit_a] = reduce_near(inner, 1, unit_a, left)
         rs_own[...] = part(0)
         return far, near
 
     def reduce_relay(state, inner):
         far, near = state
-        far[0].wait_recv()
-        rs_out[inner, 0, 0:4] = (rs_keep[0] + rs_rel[inner, 0].astype(f32)).astype(bf16)
-        near.append(copy(rs_out.at[inner, 0, 0:4], rs_in.at[inner, 0, 0:4], z, right))
-        far[1].wait_recv()
-        rs_out[inner, 1, 4:8] = (rs_keep[1] + rs_rel[inner, 1].astype(f32)).astype(bf16)
-        near.append(copy(rs_out.at[inner, 1, 4:8], rs_in.at[inner, 1, 4:8], z, left))
+        near[0, unit_a] = reduce_pass(inner, 0, unit_a, right, far[unit_a])
+        near[1, unit_c] = reduce_pass(inner, 1, unit_c, left, far[unit_c])
+        near[0, unit_d] = reduce_near(inner, 0, unit_d, right)
+        near[1, unit_b] = reduce_near(inner, 1, unit_b, left)
+        near[0, unit_b] = reduce_pass(inner, 0, unit_b, right, far[unit_b])
+        near[1, unit_d] = reduce_pass(inner, 1, unit_d, left, far[unit_d])
         return near
 
-    def reduce_column(copies, inner):
-        for c in copies:
-            c.wait_recv()
-        total = rs_own[...] + rs_in[inner, 0].astype(f32) + rs_in[inner, 1].astype(f32)
-        rs2_send[inner] = total.astype(bf16)
-        return [
-            copy(rs2_send.at[inner, flip(col, k)], rs2_recv.at[inner, k], z, peer(k))
-            for k in range(1, 8)
-        ]
+    def reduce_column(near, inner):
+        out = [None] * 7
+        for r in (unit_a, unit_c, unit_b, unit_d):
+            at = unit(r)
+            near[0, r].wait_recv()
+            near[1, r].wait_recv()
+            total = rs_own[at] + rs_in[inner, 0, at].astype(f32) + rs_in[inner, 1, at].astype(f32)
+            rs2_send[inner, at] = total.astype(bf16)
+            for k in (2 * r, 2 * r + 1):
+                if k:
+                    out[k - 1] = copy(rs2_send.at[inner, flip(col, k)], rs2_recv.at[inner, k], z, peer(k))
+        return out
 
     def reduce_quarter(copies, inner, kk):
         copies[kk + 3].wait_recv()
@@ -432,16 +473,6 @@
     usend[...] = u2.astype(bf16).reshape(8, 32, PX)
     us = [copy(usend.at[flip(g, k // 4)], urecv.at[n + 1], z, peer(k)) for n, k in enumerate(g_masks)]
     r1 = reduce_relay(r1, 0)
-    for b in range(GRP):
-        v = fb_in[CH_DEV * b : CH_DEV * (b + 1), :]
-        v = jnp.concatenate([v, jnp.zeros((CB - CH_DEV, BASIS), f32)], axis=0)
-        top = v.astype(bf16)
-        fbp[0, CB * b : CB * (b + 1), :] = top
-        fbp[1, CB * b : CB * (b + 1), :] = (v - top.astype(f32)).astype(bf16)
-    xb = dot_tn(fbp[0], x_rows) + dot_tn(fbp[1], x_rows)
-    xb_top = xb.astype(bf16)
-    xbt[0:BASIS, :] = xb_top
-    xbt[BASIS:, :] = (xb - xb_top.astype(f32)).astype(bf16)
     ex_row = sigmoid(
         split_left(dot_nt, squeeze, ex_w)
         + split_right(
@@ -465,6 +496,8 @@
     ball[me] = bq[m]
     bring = ring_start(back_copies, ball, block)
     brows = ring_relay(bring, ball, block)
+    for q in range(4):
+        bo_out[q] = dot_tn(bo[q], eye).astype(bf16)
     for c in us:
         c.wait_recv()
     u_own = usend[g].astype(f32)
@@ -500,6 +533,11 @@
     excite_back = sums_finish(se_, ez)
     sig_back = excite_back * ex_row * (1.0 - ex_row)
     be = squeeze_start(split_left(dot, sig_back, ex_w), eb8)
+    for c in c2g:
+        c.wait_recv()
+    c2 = c2s[m].astype(f32) + c2r[1].astype(f32) + c2r[2].astype(f32) + c2r[3].astype(f32)
+    c2z[...] = c2.astype(bf16)
+    c2t = [copy(c2z, c2zr.at[k], flip(z, k), me) for k in range(1, 8)]
     halo_finish(exta, halo_a)
     squeeze_back = squeeze_finish(be, eb8) * slope(squeeze_pre)
     means_back = split_right(dot_nt, sq_w, squeeze_back)
@@ -530,17 +568,11 @@
         pre[r : r + 16, :] = acc * slope(pre[r : r + 16, :])
     unpack = packing((GP, CI), 1)
     ag = dot(unpack, pre[...].astype(bf16)).astype(bf16)
-    r2 = reduce_start(w1g, ag, 1)
-
     c1 = dot_nt(ag, xbt[0:BASIS, :]) + dot_nt(ag, xbt[BASIS:, :])
     c1s[...] = c1.astype(bf16).reshape(4, CB, BASIS)
     c1g = [copy(c1s.at[flip(m, k)], c1r.at[k], z, peer(k)) for k in range(1, 4)]
-    for c in c2g:
-        c.wait_recv()
-    c2 = c2s[m].astype(f32) + c2r[1].astype(f32) + c2r[2].astype(f32) + c2r[3].astype(f32)
-    c2z[...] = c2.astype(bf16)
-    c2t = [copy(c2z, c2zr.at[k], flip(z, k), me) for k in range(1, 8)]
-    r2 = reduce_relay(r2, 1)
+    r2 = reduce_start(w1g, ag, 1)
+
     for c in hsw:
         c.wait_recv()
     grads = dot_nt(hbs[m], cols[0])
@@ -554,6 +586,7 @@
         zf[k] = both[:, ZC * k : ZC * (k + 1)]
         zs[k] = both[:, ZC * k : ZC * (k + 1)].astype(bf16)
     z1 = [copy(zs.at[flip(z, k)], zr.at[k], flip(z, k), me) for k in range(1, 8)]
+    r2 = reduce_relay(r2, 1)
     for c in c2t:
         c.wait_recv()
     c2 = c2z[...].astype(f32)
@@ -579,7 +612,7 @@
     c2rows = ring_relay(c2ring, c2all, slot2, same)
     for kk in range(4):
         q = flip(m, kk)
-        ig[q] = (bq[q].astype(f32) + reduce_quarter(c2cols, 1, kk)).astype(bf16)
+        ig_out[q] = dot_tn((bq[q].astype(f32) + reduce_quarter(c2cols, 1, kk)).astype(bf16), eye).astype(bf16)
     swaps = [copy(c2all.at[slot2(me, k)], c2all.at[slot2(me, k)], z, peer(1)) for k in same]
     for c in c2rows:
         c.wait_recv()
@@ -640,17 +673,13 @@
     first_basis,
     second_basis,
 ):
-    def quarters(v):
-        v = v.reshape(2, 2, PX, CH_DEV).transpose(0, 1, 3, 2)
-        return jnp.pad(v, ((0, 0), (0, 0), (0, CB - CH_DEV), (0, 0))).reshape(4, CB, PX)
-
-    xq, cq = quarters(inputs), quarters(cotangent)
-    biases = jnp.pad(jnp.stack([first_bias, conv_bias, excite_bias]), ((0, 5), (0, SQP - CH_DEV)))
-    squeeze_rows = jnp.broadcast_to(jnp.pad(squeeze_bias, (0, SQP - SQ))[None], (8, SQP))
-    side = jnp.concatenate([squeeze_rows, biases])
-
     V = pltpu.VMEM
     scratch = [
+        V((4, CB, PX), bf16),
+        V((4, CB, PX), bf16),
+        V((NCH, BASIS), f32),
+        V((8, 128), f32),
+        V((8, SQP), f32),
         V((GRP, CB, PX), bf16),
         V((GRP, CB, PX), bf16),
         V((CB, RAW), bf16),
@@ -680,9 +709,10 @@
         V((GP, PX), f32),
         V((2 * BASIS, PX), bf16),
         V((AP, 512), f32),
+        V((4, CB, PX), bf16),
         V((2, 8, CB, PX), bf16),
-        V((2, 2, 4, CB, PX), bf16),
-        V((2, 4, CB, PX), f32),
+        V((2, 8, CB, PX), bf16),
+        V((2, 8, CB, PX), f32),
         V((2, 2, 8, CB, PX), bf16),
         V((2, 2, 8, CB, PX), bf16),
         V((8, CB, PX), f32),
@@ -719,30 +749,28 @@
     bo, ig, fg, sg, cg, sqg, exg = pl.pallas_call(
         body,
         out_shape=[
-            shape((4, CB, PX), bf16),
-            shape((4, CB, PX), bf16),
+            shape((4, PX, CH_DEV), bf16),
+            shape((4, PX, CH_DEV), bf16),
             shape((CH_DEV, NCH), f32),
             shape((CH_DEV, NCH), f32),
             shape((9, CH_DEV, 264), f32),
             shape((CH_DEV, SQ), f32),
             shape((CH_DEV, SQ), f32),
         ],
-        in_specs=[spec] * 10,
+        in_specs=[spec] * 8 + [pl.BlockSpec(memory_space=pl.ANY)] + [spec] * 4,
         out_specs=[spec] * 7,
         scratch_shapes=scratch,
         compiler_params=pltpu.CompilerParams(
             collective_id=0, has_side_effects=True, vmem_limit_bytes=62 * 1024 * 1024
         ),
     )(
-        xq, cq, first_weight.T, conv_weight.transpose(1, 0, 2), second_weight,
-        squeeze_weight, excite_weight.T, second_basis, first_basis, side,
+        inputs.reshape(4, PX, CH_DEV), cotangent.reshape(4, PX, CH_DEV),
+        first_weight.T, conv_weight.transpose(1, 0, 2), second_weight,
+        squeeze_weight, excite_weight.T, second_basis, first_basis,
+        first_bias[None], conv_bias[None], excite_bias[None], squeeze_bias[None],
     )
 
-    def pixels(v):
-        v = v[:, :CH_DEV].reshape(2, 2, CH_DEV, PX).transpose(0, 1, 3, 2)
-        return v.reshape(inputs.shape)
-
-    return (pixels(bo), pixels(ig), fg.T, sg, cg.transpose(1, 0, 2), sqg, exg.T)
+    return (bo.reshape(inputs.shape), ig.reshape(inputs.shape), fg.T, sg, cg.transpose(1, 0, 2), sqg, exg.T)
 
 
 def solution(mesh):

time: 171 us -> 162 us (0.947); the launches traced: 171 us -> 159 us
  Pallas kernels: 156 us -> 148 us
  local copies, waits for them, and re-layouts: 13.1 us -> 9.86 us
    pallas_call x1, Pallas kernels: 156 us -> 148 us  [per_device(): pl.pallas_call(body, out_shape=[shape((4, PX, CH_DEV), bf16), shape((4, P...]
    unnamed x13 -> x15, local copies, waits for them, and re-layouts: 5.13 us -> 8.59 us
    reshape x2 -> x0, local copies, waits for them, and re-layouts: 2.21 us -> none  [quarters(): v = v.reshape(2, 2, PX, CH_DEV).transpose(0, 1, 3, 2)]
    pad x3 -> x0, local copies, waits for them, and re-layouts: 2.06 us -> none  [the longest x2 1.37 us: quarters(): jnp.pad(v, ((0, 0), (0, 0), (0, CB - CH_DEV), (0, 0))).reshape(4, CB, PX)]
    slice x2 -> x0, local copies, waits for them, and re-layouts: 1.96 us -> none  [pixels(): v = v[:, :CH_DEV].reshape(2, 2, CH_DEV, PX).transpose(0, 1, 3, 2)]
    transpose x2 -> x0, local copies, waits for them, and re-layouts: 1.73 us -> none  [pixels(): v = v[:, :CH_DEV].reshape(2, 2, CH_DEV, PX).transpose(0, 1, 3, 2)]
where the time goes in v3:
time: 162 us; the launch traced here: 159 us
  Pallas kernels  148 us (91%)
  local copies, waits for them, and re-layouts  9.86 us (6%)
    pallas_call x1, Pallas kernels, per_device(): pl.pallas_call(body, out_shape=[shape((4, PX, CH_DEV), bf16), shape((4, P...  148 us
    unnamed x15, local copies, waits for them, and re-layouts  8.59 us

profile of v3, /device:TPU:2, one launch (start us, length us, event | category | flops | bytes accessed | tf_op | source)
XLA Modules:
  0.0 158.9 jit_solution(12374272647258963630)
XLA Ops:
  0.6 1.3 broadcast_in_dim.15.b4
  1.9 148.4 %shard_map.180 = (bf16[4,256,66]{2,1,0:T(8,128)(2,1)}, bf16[4,256,66]{2,1,0:T(8,128)(2,1)}, f32[66,2112]{1,0:T(8,128)}, f32[66,2112]{1,0:T(8,128)}, f32[9,66,264...) custom-call(bf16[4,256,66]{2,1,0:T(8,128)(2,1)} %bitcast.17, bf16[4,256,66]{2,1,0:T(8,128)(2,1)} %bitcast.18, ...), custom_call_target="tpu_custom_call" | custom-call | tf_op jit(solution)/shard_map/pallas_call | solution.py:749
  150.3 0.0 copy-start.1
  150.3 0.0 copy-start
  150.3 1.8 %copy.27 = bf16[2,8,64,66]{3,2,1,0:T(8,128)(2,1)} copy(bf16[2,8,64,66]{3,2,1,0:T(8,128)(2,1)} %bitcast.20) | data formatting | bytes 270336
  152.1 1.7 %copy.28 = bf16[2,8,64,66]{3,2,1,0:T(8,128)(2,1)} copy(bf16[2,8,64,66]{3,2,1,0:T(8,128)(2,1)} %bitcast.19) | data formatting | bytes 270336
  153.8 0.0 copy-start.3
  153.8 0.0 copy-start.2
  153.8 2.0 %copy.29 = f32[2112,66]{0,1:T(8,128)} copy(f32[2112,66]{0,1:T(8,128)} %bitcast.14) | data formatting | bytes 1115136
  155.8 0.0 copy-done.1
  155.8 0.8 copy.30
  156.6 0.0 copy-done
  156.6 0.9 copy.31
  157.6 0.0 copy-done.3
  157.6 0.7 copy.32
  158.2 0.0 copy-done.2
  158.2 0.7 copy.33
Async XLA Ops:
  150.3 5.5 %copy-start.1 = (f32[66,2112]{1,0:T(8,128)S(1)}, f32[66,2112]{1,0:T(8,128)}, u32[]{:S(2)}) copy-start(f32[66,2112]{1,0:T(8,128)} %get-tuple-element.31) | copy-start | bytes 1672708
  150.3 6.3 %copy-start = (f32[9,66,264]{2,1,0:T(8,128)S(1)}, f32[9,66,264]{2,1,0:T(8,128)}, u32[]{:S(2)}) copy-start(f32[9,66,264]{2,1,0:T(8,128)} %get-tuple-element.18) | copy-start | bytes 1881796
  153.8 3.8 %copy-start.3 = (f32[66,528]{1,0:T(8,128)S(1)}, f32[66,528]{1,0:T(8,128)}, u32[]{:S(2)}) copy-start(f32[66,528]{1,0:T(8,128)} %get-tuple-element.33) | copy-start | bytes 418180
  153.8 4.5 %copy-start.2 = (f32[66,528]{1,0:T(8,128)S(1)}, f32[66,528]{1,0:T(8,128)}, u32[]{:S(2)}) copy-start(f32[66,528]{1,0:T(8,128)} %get-tuple-element.20) | copy-start | bytes 418180

commit v4 on v3

--- a/solution.py
+++ b/solution.py
@@ -96,12 +96,12 @@
 def body(
     x_in, c_in, w1, wc, w2, sqw, exw, sb_in, fb_hbm, b1, b2, b3, b4,
     bo_out, ig_out, fg, sg, cg, sqg, exg,
-    xq, cq, fb_in, bt, sqb, xall, ball, w1p, w2p, wcp, smp, bip, w1r, w2r, w1g, wcg, w2g, smg, big,
+    xq, cq, fb_in, bt, sqb, xall, ball, w1p, w2p, wcp, smp, sbp, bip, w1r, w2r, w1g, wcg, w2g, smg, sbg, big,
     hots, hots2, fbp, fbn,
     ext, extg, exts, exta, cols, pre, conv_out, hidden, sback, xbt, zbuf,
     bo, rs_far, rs_rel, rs_keep, rs_out, rs_in, rs_own, rs2_send, rs2_recv, bq,
     usend, urecv, c2s, c2r, c2z, c2zr, c2all,
-    hs, hz, hb8, es, ez, eb8, hbs, hbr, c1s, c1r, zs, zf, zr, zall,
+    sls, slr, gs, ga, mb_all, hs, hz, hb8, es, ez, eb8, hbs, hbr, c1s, c1r, zs, zf, zr, zall,
     send, recv, local,
 ):
     z = lax.axis_index("tile")
@@ -116,15 +116,19 @@
     started = []
     locals_ = []
 
-    def copy(src, dst, tile, grp):
+    def later(src, dst, tile, grp):
         i = count[0]
         count[0] += 1
         c = pltpu.make_async_remote_copy(
             src_ref=src, dst_ref=dst, send_sem=send.at[i], recv_sem=recv.at[i],
             device_id=(tile, grp), device_id_type=MESH,
         )
+        started.append(c)
+        return c
+
+    def copy(src, dst, tile, grp):
+        c = later(src, dst, tile, grp)
         c.start()
-        started.append(c)
         return c
 
     def keep(src, dst):
@@ -248,17 +252,6 @@
         hots[n] = one_hot(512, low, 256, start, CB, CH_DEV)
     s1 = group_forward(s1, w1r)
     sbi = group_forward(sbi, big)
-    smp[...] = jnp.zeros(smp.shape, bf16)
-    smp[0:CH_DEV, 0:SQ] = sqw[...]
-    smp[0:CH_DEV, SQP : SQP + SQ] = exw[...]
-    sb = sb_in[...]
-    sb_top = sb.astype(bf16)
-    smp[0:CH_DEV, 2 * SQP : 2 * SQP + BASIS] = sb_top
-    smp[0:CH_DEV, 2 * SQP + BASIS :] = (sb - sb_top.astype(f32)).astype(bf16)
-    w2p[...] = jnp.zeros(w2p.shape, bf16)
-    w2p[0:CH_DEV, 0:NCH] = w2[...]
-    for q in range(4):
-        cq[q] = dot_nt(eye, c_in[q]).astype(bf16)
 
     def packing(shape, packed_dim):
         row = lax.broadcasted_iota(jnp.int32, shape, packed_dim)
@@ -282,8 +275,19 @@
     ext[1] = packed[:, 0:128]
     ext[2] = packed[:, 128:256]
     halo = halo_start(ext)
+    smp[...] = jnp.zeros(smp.shape, bf16)
+    smp[0:CH_DEV, 0:SQ] = sqw[...]
+    smp[0:CH_DEV, SQP : SQP + SQ] = exw[...]
     ssm = group_start(smp, smg)
+    w2p[...] = jnp.zeros(w2p.shape, bf16)
+    w2p[0:CH_DEV, 0:NCH] = w2[...]
     s2 = group_start(w2p, w2r)
+    sb = sb_in[...]
+    sb_top = sb.astype(bf16)
+    sbp[...] = jnp.zeros(sbp.shape, bf16)
+    sbp[0:CH_DEV, 0:BASIS] = sb_top
+    sbp[0:CH_DEV, BASIS:] = (sb - sb_top.astype(f32)).astype(bf16)
+    ssb = group_start(sbp, sbg)
     pre[...] = split_right(dot, pack, first_pre)
     sc = group_forward(sc, wcg)
     for k in range(4):
@@ -368,7 +372,6 @@
     ssm = group_forward(ssm, smg)
     sext = group_start(ext, extg)
     sh = sums_tiles(ah, hs, hz)
-    s2 = group_forward(s2, w2r)
     group_finish(ssm)
     fb_copy.wait()
     for b in range(GRP):
@@ -381,6 +384,9 @@
     sq_w = smg[:, :, 0:SQP].reshape(GP, SQP)
     ex_w = smg[:, :, SQP : 2 * SQP].reshape(GP, SQP)
     bh = squeeze_start(split_left(dot, means, sq_w), hb8)
+    for q in range(4):
+        cq[q] = dot_nt(eye, c_in[q]).astype(bf16)
+    s2 = group_forward(s2, w2r)
     group_finish(s2)
     spread(w2r, w2g)
     xb = dot_tn(fbp[0], x_rows) + dot_tn(fbp[1], x_rows)
@@ -466,13 +472,16 @@
     for n in range(2):
         exts[n + 1] = sl[:, 128 * n : 128 * (n + 1)]
     halo_s = halo_start(exts)
-    sext = group_forward(sext, extg)
-    sb_top = smg[:, :, 2 * SQP : 2 * SQP + BASIS].reshape(GP, BASIS)
-    sb_low = smg[:, :, 2 * SQP + BASIS :].reshape(GP, BASIS)
+    sls[...] = sl.reshape(4, CB, PX)
+    ssl = [copy(sls.at[flip(m, k)], slr.at[k], z, peer(k)) for k in range(1, 4)]
+    r1 = reduce_relay(r1, 0)
+    ssb = group_forward(ssb, sbg)
+    group_finish(ssb)
+    sb_top = sbg[:, :, 0:BASIS].reshape(GP, BASIS)
+    sb_low = sbg[:, :, BASIS:].reshape(GP, BASIS)
     u2 = dot_tn(sb_top, scaled) + dot_tn(sb_low, scaled)
     usend[...] = u2.astype(bf16).reshape(8, 32, PX)
     us = [copy(usend.at[flip(g, k // 4)], urecv.at[n + 1], z, peer(k)) for n, k in enumerate(g_masks)]
-    r1 = reduce_relay(r1, 0)
     ex_row = sigmoid(
         split_left(dot_nt, squeeze, ex_w)
         + split_right(
@@ -483,6 +492,7 @@
     )
     halo_finish(exts, halo_s)
     c2cols = reduce_column(r1, 0)
+    sext = group_forward(sext, extg)
     back_copies = [None] * 7
     for kk in range(4):
         q = flip(m, kk)
@@ -513,6 +523,10 @@
         return carry
 
     lax.fori_loop(1, 4, build_other, 0)
+    for c in ssl:
+        c.wait_recv()
+    gs[0] = dot_nt(sls[m], cols[0]) + dot_nt(slr[1], cols[1])
+    gs[1] = dot_nt(slr[2], cols[2]) + dot_nt(slr[3], cols[3])
     for c in brows:
         c.wait_recv()
 
@@ -525,11 +539,19 @@
     for n in range(2):
         exta[n + 1] = edge[:, 128 * n : 128 * (n + 1)]
     halo_a = halo_start(exta)
+    hbs[...] = (scaled_back * slope(conv_out[...])).astype(bf16).reshape(4, CB, PX)
+    hsw = [copy(hbs.at[flip(m, k)], hbr.at[k], z, peer(k)) for k in range(1, 4)]
     se_ = sums_tiles(ae, es, ez)
     coords = dot_nt(u_top, back_rows) + dot_nt(u_low, back_rows)
     for k in range(4):
         c2s[k] = coords[:, 640 * k : 640 * (k + 1)].astype(bf16)
     c2g = [copy(c2s.at[flip(m, k)], c2r.at[k], z, peer(k)) for k in range(1, 4)]
+    for c in hsw:
+        c.wait_recv()
+    acc = dot_nt(hbs[m], cols[0])
+    for k in range(1, 4):
+        acc = acc + dot_nt(hbr[k], cols[k])
+    ga[...] = acc
     excite_back = sums_finish(se_, ez)
     sig_back = excite_back * ex_row * (1.0 - ex_row)
     be = squeeze_start(split_left(dot, sig_back, ex_w), eb8)
@@ -543,8 +565,20 @@
     means_back = split_right(dot_nt, sq_w, squeeze_back)
     mb_col = jnp.where(img == 0, means_back[:, 0:1], means_back[:, 1:2]) * (1.0 / CELLS)
     hb = ((sback[...] + mb_col) * slope(conv_out[...])).astype(bf16)
-    hbs[...] = hb.reshape(4, CB, PX)
-    hsw = [copy(hbs.at[flip(m, k)], hbr.at[k], z, peer(k)) for k in range(1, 4)]
+    mb_all[...] = means_back
+    mb_own = mb_all[pl.ds(pl.multiple_of(CB * m, 16), CB), :] * (1.0 / CELLS)
+    mb_same = jnp.where(img == 0, mb_own[:, 0:1], mb_own[:, 1:2])
+    mb_far = jnp.where(img == 0, mb_own[:, 1:2], mb_own[:, 0:1])
+    grads = ga[...] + mb_same * gs[0] + mb_far * gs[1]
+    for k in range(TILES - 2):
+        zf[k] = grads[:, ZC * k : ZC * (k + 1)]
+        zs[k] = grads[:, ZC * k : ZC * (k + 1)].astype(bf16)
+    tail = grads[:, ZC * (TILES - 2) :]
+    z1 = []
+    for k in range(1, 8):
+        there = flip(z, k)
+        z1.append(later(zs.at[there], zr.at[k], there, me))
+        pl.when(there < TILES - 2)(z1[-1].start)
     before, after = [
         ((exta[n].astype(f32) + mb_col) * exts[n].astype(f32)).astype(bf16) for n in (0, 3)
     ]
@@ -573,19 +607,16 @@
     c1g = [copy(c1s.at[flip(m, k)], c1r.at[k], z, peer(k)) for k in range(1, 4)]
     r2 = reduce_start(w1g, ag, 1)
 
-    for c in hsw:
-        c.wait_recv()
-    grads = dot_nt(hbs[m], cols[0])
-    for k in range(1, 4):
-        grads = grads + dot_nt(hbr[k], cols[k])
     for c in c1g:
         c.wait_recv()
     c1 = c1s[m].astype(f32) + c1r[1].astype(f32) + c1r[2].astype(f32) + c1r[3].astype(f32)
-    both = jnp.concatenate([grads, c1, jnp.zeros((CB, TILES * ZC - AP - BASIS), f32)], axis=1)
-    for k in range(TILES):
-        zf[k] = both[:, ZC * k : ZC * (k + 1)]
-        zs[k] = both[:, ZC * k : ZC * (k + 1)].astype(bf16)
-    z1 = [copy(zs.at[flip(z, k)], zr.at[k], flip(z, k), me) for k in range(1, 8)]
+    both = jnp.concatenate([tail, c1, jnp.zeros((CB, TILES * ZC - AP - BASIS), f32)], axis=1)
+    for k in (TILES - 2, TILES - 1):
+        part = both[:, ZC * (k - TILES + 2) : ZC * (k - TILES + 3)]
+        zf[k] = part
+        zs[k] = part.astype(bf16)
+    for k in range(1, 8):
+        pl.when(flip(z, k) >= TILES - 2)(z1[k - 1].start)
     r2 = reduce_relay(r2, 1)
     for c in c2t:
         c.wait_recv()
@@ -639,8 +670,8 @@
     for c in swaps:
         c.wait_recv()
     wide = jnp.concatenate([c2all[8 * k : 8 * (k + 1)].reshape(BASIS, 640) for k in range(4)], axis=1)
-    own_top = smp[:, 2 * SQP : 2 * SQP + BASIS]
-    own_low = smp[:, 2 * SQP + BASIS :]
+    own_top = sbp[:, 0:BASIS]
+    own_low = sbp[:, BASIS:]
     for n, (start, width, low) in enumerate(windows(NCH, CH_DEV, AP, CB)):
         v = dot(wide[:, low : low + 512], hots2[n]).astype(bf16)
         v = (dot(own_top, v) + dot(own_low, v)) * GRAD_SCALE
@@ -656,6 +687,15 @@
         cg[t] = sums[0:CH_DEV, CI * t : CI * t + 264]
     for c in started:
         c.wait_send()
+
+
+def copy_out(*refs):
+    sems = refs[14]
+    copies = [pltpu.make_async_copy(refs[n], refs[n + 7], sems.at[n]) for n in range(7)]
+    for c in copies:
+        c.start()
+    for c in copies:
+        c.wait()
 
 
 def per_device(
@@ -685,14 +725,16 @@
         V((CB, RAW), bf16),
         V((CB, RAW), bf16),
         V((CB, AP), bf16),
-        V((CB, 2 * SQP + 2 * BASIS), bf16),
+        V((CB, 2 * SQP), bf16),
+        V((CB, 2 * BASIS), bf16),
         V((CB, 128), f32),
         V((4, CB, RAW), bf16),
         V((4, CB, RAW), bf16),
         V((GP, AP), bf16),
         V((4, CB, AP), bf16),
         V((GP, AP), bf16),
-        V((4, CB, 2 * SQP + 2 * BASIS), bf16),
+        V((4, CB, 2 * SQP), bf16),
+        V((4, CB, 2 * BASIS), bf16),
         V((4, CB, 128), f32),
         V((10, 512, 256), bf16),
         V((9, 512, 256), bf16),
@@ -726,6 +768,11 @@
         V((32, 640), bf16),
         V((8, 32, 640), bf16),
         V((32, 32, 640), bf16),
+        V((4, CB, PX), bf16),
+        V((4, CB, PX), bf16),
+        V((2, CB, AP), f32),
+        V((CB, AP), f32),
+        V((GP, 8), f32),
         V((4, 8, 128), f32),
         V((8, 8, 128), f32),
         V((8, 2, 8, 128), f32),
@@ -770,6 +817,14 @@
         first_bias[None], conv_bias[None], excite_bias[None], squeeze_bias[None],
     )
 
+    results = (bo, ig, fg, sg, cg, sqg, exg)
+    bo, ig, fg, sg, cg, sqg, exg = pl.pallas_call(
+        copy_out,
+        out_shape=[shape(v.shape, v.dtype) for v in results],
+        in_specs=[pl.BlockSpec(memory_space=pl.ANY)] * 7,
+        out_specs=[pl.BlockSpec(memory_space=pl.ANY)] * 7,
+        scratch_shapes=[pltpu.SemaphoreType.DMA((7,))],
+    )(*results)
     return (bo.reshape(inputs.shape), ig.reshape(inputs.shape), fg.T, sg, cg.transpose(1, 0, 2), sqg, exg.T)
 
 

time: 162 us -> 247 us (1.52)
  Pallas kernels: 148 us -> 243 us
  local copies, waits for them, and re-layouts: 9.86 us -> 1.27 us
    pallas_call x0 -> x1, Pallas kernels: none -> 96.3 us  [per_device(): pl.pallas_call(copy_out, out_shape=[shape(v.shape, v.dtype) for v in resu...]
    unnamed x15 -> x0, local copies, waits for them, and re-layouts: 8.59 us -> none
where the time goes in v4:
time: 247 us; the launch traced here: 245 us
  Pallas kernels  243 us (98%)
    pallas_call x1, Pallas kernels, per_device(): pl.pallas_call(body, out_shape=[shape((4, PX, CH_DEV), bf16), shape((4, P...  147 us
    pallas_call x1, Pallas kernels, per_device(): pl.pallas_call(copy_out, out_shape=[shape(v.shape, v.dtype) for v in resu...  96.3 us

profile of v4, /device:TPU:2, one launch (start us, length us, event | category | flops | bytes accessed | tf_op | source)
XLA Modules:
  0.0 245.5 jit_solution(8025980698005292085)
XLA Ops:
  0.6 1.3 broadcast_in_dim.15.b4
  1.9 147.1 %shard_map.180 = (bf16[4,256,66]{2,1,0:T(8,128)(2,1)}, bf16[4,256,66]{2,1,0:T(8,128)(2,1)}, f32[66,2112]{1,0:T(8,128)}, f32[66,2112]{1,0:T(8,128)}, f32[9,66,264...) custom-call(bf16[4,256,66]{2,1,0:T(8,128)(2,1)} %bitcast.15, bf16[4,256,66]{2,1,0:T(8,128)(2,1)} %bitcast.16, ...), custom_call_target="tpu_custom_call" | custom-call | tf_op jit(solution)/shard_map/pallas_call | solution.py:796
  149.0 96.3 %shard_map.181 = (bf16[4,256,66]{2,1,0:T(8,128)(2,1)}, bf16[4,256,66]{2,1,0:T(8,128)(2,1)}, f32[66,2112]{1,0:T(8,128)}, f32[66,2112]{1,0:T(8,128)}, f32[9,66,264...) custom-call(bf16[4,256,66]{2,1,0:T(8,128)(2,1)} %get-tuple-element.21.refs_0_, ...), custom_call_target="tpu_custom_call" | custom-call | tf_op jit(solution)/shard_map/pallas_call | solution.py:821

commit v5 on v4

--- a/solution.py
+++ b/solution.py
@@ -607,6 +607,19 @@
     c1g = [copy(c1s.at[flip(m, k)], c1r.at[k], z, peer(k)) for k in range(1, 4)]
     r2 = reduce_start(w1g, ag, 1)
 
+    for c in c2t:
+        c.wait_recv()
+    c2 = c2z[...].astype(f32)
+    for k in range(1, 8):
+        c2 = c2 + c2zr[k].astype(f32)
+
+    def slot2(device, k):
+        d = flip(device, k)
+        return (d % 4) * 8 + d // 4
+
+    same = (0, 2, 4, 6)
+    c2all[slot2(me, 0)] = c2.astype(bf16)
+    c2c = gather_column(lambda k: c2all.at[slot2(me, 0)], c2all, slot2, same[1:])
     for c in c1g:
         c.wait_recv()
     c1 = c1s[m].astype(f32) + c1r[1].astype(f32) + c1r[2].astype(f32) + c1r[3].astype(f32)
@@ -618,21 +631,9 @@
     for k in range(1, 8):
         pl.when(flip(z, k) >= TILES - 2)(z1[k - 1].start)
     r2 = reduce_relay(r2, 1)
-    for c in c2t:
-        c.wait_recv()
-    c2 = c2z[...].astype(f32)
-    for k in range(1, 8):
-        c2 = c2 + c2zr[k].astype(f32)
-
-    def slot2(device, k):
-        d = flip(device, k)
-        return (d % 4) * 8 + d // 4
-
-    same = (0, 2, 4, 6)
-    c2all[slot2(me, 0)] = c2.astype(bf16)
-    c2c = gather_column(lambda k: c2all.at[slot2(me, 0)], c2all, slot2, same[1:])
+    c2ring = ring_start(c2c, c2all, slot2, same)
+    swaps = [copy(c2all.at[slot2(me, k)], c2all.at[slot2(me, k)], z, peer(1)) for k in same]
     c2cols = reduce_column(r2, 1)
-    c2ring = ring_start(c2c, c2all, slot2, same)
     for c in z1:
         c.wait_recv()
     chunk = zf[z]
@@ -644,7 +645,6 @@
     for kk in range(4):
         q = flip(m, kk)
         ig_out[q] = dot_tn((bq[q].astype(f32) + reduce_quarter(c2cols, 1, kk)).astype(bf16), eye).astype(bf16)
-    swaps = [copy(c2all.at[slot2(me, k)], c2all.at[slot2(me, k)], z, peer(1)) for k in same]
     for c in c2rows:
         c.wait_recv()
     for step in (1, 2, 3):
@@ -690,12 +690,8 @@
 
 
 def copy_out(*refs):
-    sems = refs[14]
-    copies = [pltpu.make_async_copy(refs[n], refs[n + 7], sems.at[n]) for n in range(7)]
-    for c in copies:
-        c.start()
-    for c in copies:
-        c.wait()
+    for source, target in zip(refs[:7], refs[7:]):
+        target[...] = source[...]
 
 
 def per_device(
@@ -821,9 +817,9 @@
     bo, ig, fg, sg, cg, sqg, exg = pl.pallas_call(
         copy_out,
         out_shape=[shape(v.shape, v.dtype) for v in results],
-        in_specs=[pl.BlockSpec(memory_space=pl.ANY)] * 7,
-        out_specs=[pl.BlockSpec(memory_space=pl.ANY)] * 7,
-        scratch_shapes=[pltpu.SemaphoreType.DMA((7,))],
+        in_specs=[spec] * 7,
+        out_specs=[spec] * 7,
+        compiler_params=pltpu.CompilerParams(vmem_limit_bytes=32 * 1024 * 1024),
     )(*results)
     return (bo.reshape(inputs.shape), ig.reshape(inputs.shape), fg.T, sg, cg.transpose(1, 0, 2), sqg, exg.T)
 

time: 247 us -> 160 us (0.65)
  Pallas kernels: 243 us -> 150 us
  local copies, waits for them, and re-layouts: 1.27 us -> 8.36 us
    pallas_call x1, Pallas kernels: 96.3 us -> 1.91 us  [per_device(): pl.pallas_call(copy_out, out_shape=[shape(v.shape, v.dtype) for v in resu...]
    unnamed x0 -> x14, local copies, waits for them, and re-layouts: none -> 7.1 us
where the time goes in v5:
time: 160 us; the launch traced here: 159 us
  Pallas kernels  150 us (94%)
  local copies, waits for them, and re-layouts  8.36 us (5%)
    pallas_call x1, Pallas kernels, per_device(): pl.pallas_call(body, out_shape=[shape((4, PX, CH_DEV), bf16), shape((4, P...  148 us
    unnamed x14, local copies, waits for them, and re-layouts  7.1 us

profile of v5, /device:TPU:2, one launch (start us, length us, event | category | flops | bytes accessed | tf_op | source)
XLA Modules:
  0.0 158.6 jit_solution(3582367395822641103)
XLA Ops:
  0.6 1.3 broadcast_in_dim.15.b4
  1.9 147.7 %shard_map.180 = (bf16[4,256,66]{2,1,0:T(8,128)(2,1)}, bf16[4,256,66]{2,1,0:T(8,128)(2,1)}, f32[66,2112]{1,0:T(8,128)}, f32[66,2112]{1,0:T(8,128)}, f32[9,66,264...) custom-call(bf16[4,256,66]{2,1,0:T(8,128)(2,1)} %bitcast.15, bf16[4,256,66]{2,1,0:T(8,128)(2,1)} %bitcast.16, ...), custom_call_target="tpu_custom_call" | custom-call | tf_op jit(solution)/shard_map/pallas_call | solution.py:792
  149.6 0.0 copy-start
  149.6 1.2 copy-done
  150.8 0.0 copy-start.1
  150.8 1.1 copy-done.1
  151.9 0.0 copy-start.2
  151.9 1.1 copy-done.2
  152.9 0.0 copy-start.3
  152.9 0.9 copy-done.3
  153.9 0.0 copy-start.4
  153.9 0.9 copy-done.4
  154.8 0.0 copy-start.5
  154.8 0.9 copy-done.5
  155.8 0.0 copy-start.6
  155.8 0.9 copy-done.6
  156.7 1.9 %shard_map.181 = (bf16[4,256,66]{2,1,0:T(8,128)(2,1)}, bf16[4,256,66]{2,1,0:T(8,128)(2,1)}, f32[66,2112]{1,0:T(8,128)}, f32[66,2112]{1,0:T(8,128)}, f32[9,66,264...) custom-call(bf16[4,256,66]{2,1,0:T(8,128)(2,1)S(1)} %copy-done.3, bf16[4,256,66]{2,1,0:T(8,128)(2,1)S(1)} %copy-done.4, ...), custom_call_target="tpu_custom_call" | custom-call | tf_op jit(solution)/shard_map/pallas_call | solution.py:817
Async XLA Ops:
  149.6 1.2 copy-start
  150.8 1.1 copy-start.1
  151.9 1.1 copy-start.2
  152.9 0.9 copy-start.3
  153.9 0.9 copy-start.4
  154.8 0.9 copy-start.5
  155.8 0.9 copy-start.6

commit v6 on v5

--- a/solution.py
+++ b/solution.py
@@ -94,9 +94,9 @@
 
 
 def body(
-    x_in, c_in, w1, wc, w2, sqw, exw, sb_in, fb_hbm, b1, b2, b3, b4,
+    x_hbm, c_hbm, w1, wc, w2, sqw, exw, sb_hbm, fb_hbm, b1_hbm, b2_hbm, b3_hbm, b4_hbm,
     bo_out, ig_out, fg, sg, cg, sqg, exg,
-    xq, cq, fb_in, bt, sqb, xall, ball, w1p, w2p, wcp, smp, sbp, bip, w1r, w2r, w1g, wcg, w2g, smg, sbg, big,
+    x_in, c_in, sb_in, b1, b2, b3, b4, xq, cq, fb_in, bt, sqb, xall, ball, w1p, w2p, wcp, smp, sbp, bip, w1r, w2r, w1g, wcg, w2g, smg, sbg, big,
     hots, hots2, fbp, fbn,
     ext, extg, exts, exta, cols, pre, conv_out, hidden, sback, xbt, zbuf,
     bo, rs_far, rs_rel, rs_keep, rs_out, rs_in, rs_own, rs2_send, rs2_recv, bq,
@@ -152,13 +152,19 @@
         pl.semaphore_signal(barrier, inc=1, device_id=(flip(z, mask), me), device_id_type=MESH)
     pl.semaphore_signal(barrier, inc=1, device_id=other, device_id_type=MESH)
 
+    x_copy = keep(x_hbm, x_in)
+    bias_copies = [keep(b1_hbm, b1), keep(b2_hbm, b2), keep(b3_hbm, b3)]
+    late_copies = [keep(b4_hbm, b4), keep(sb_hbm, sb_in), keep(c_hbm, c_in)]
     fb_copy = keep(fb_hbm, fb_in)
     diagonal = lax.broadcasted_iota(jnp.int32, (CB, CH_DEV), 0) == lax.broadcasted_iota(jnp.int32, (CB, CH_DEV), 1)
     eye = jnp.where(diagonal, 1.0, 0.0).astype(bf16)
+    w1p[...] = jnp.zeros(w1p.shape, bf16)
+    w1p[0:CH_DEV, 0:NCH] = w1[...]
+    x_copy.wait()
     for q in range(4):
         xq[q] = dot_nt(eye, x_in[q]).astype(bf16)
-    w1p[...] = jnp.zeros(w1p.shape, bf16)
-    w1p[0:CH_DEV, 0:NCH] = w1[...]
+    for c in bias_copies:
+        c.wait()
     bt[...] = jnp.zeros(bt.shape, f32)
     for n, vector in enumerate((b1, b2, b3)):
         bt[n : n + 1, 0:CH_DEV] = vector[...]
@@ -241,6 +247,8 @@
     sbi = group_start(bip, big)
     keep(xq.at[m], xall.at[me]).wait()
     xring = ring_start(xs, xall, block)
+    for c in late_copies:
+        c.wait()
     sqb[...] = jnp.zeros(sqb.shape, f32)
     sqb[0:1, 0:SQ] = b4[...]
     wcp[...] = jnp.zeros(wcp.shape, bf16)
@@ -690,8 +698,12 @@
 
 
 def copy_out(*refs):
-    for source, target in zip(refs[:7], refs[7:]):
-        target[...] = source[...]
+    sems = refs[14]
+    copies = [pltpu.make_async_copy(refs[n], refs[n + 7], sems.at[n]) for n in range(7)]
+    for c in copies:
+        c.start()
+    for c in copies:
+        c.wait()
 
 
 def per_device(
@@ -711,6 +723,13 @@
 ):
     V = pltpu.VMEM
     scratch = [
+        V((4, PX, CH_DEV), bf16),
+        V((4, PX, CH_DEV), bf16),
+        V((CH_DEV, BASIS), f32),
+        V((1, CH_DEV), f32),
+        V((1, CH_DEV), f32),
+        V((1, CH_DEV), f32),
+        V((1, SQ), f32),
         V((4, CB, PX), bf16),
         V((4, CB, PX), bf16),
         V((NCH, BASIS), f32),
@@ -785,9 +804,9 @@
         V((TILES, CB, ZC), bf16),
         pltpu.SemaphoreType.DMA((NSEM,)),
         pltpu.SemaphoreType.DMA((NSEM,)),
-        pltpu.SemaphoreType.DMA((16,)),
+        pltpu.SemaphoreType.DMA((32,)),
     ]
-    spec = pl.BlockSpec(memory_space=pltpu.VMEM)
+    spec, held = pl.BlockSpec(memory_space=pltpu.VMEM), pl.BlockSpec(memory_space=pl.ANY)
     shape = jax.ShapeDtypeStruct
     bo, ig, fg, sg, cg, sqg, exg = pl.pallas_call(
         body,
@@ -800,7 +819,7 @@
             shape((CH_DEV, SQ), f32),
             shape((CH_DEV, SQ), f32),
         ],
-        in_specs=[spec] * 8 + [pl.BlockSpec(memory_space=pl.ANY)] + [spec] * 4,
+        in_specs=[held] * 2 + [spec] * 5 + [held] * 6,
         out_specs=[spec] * 7,
         scratch_shapes=scratch,
         compiler_params=pltpu.CompilerParams(
@@ -817,9 +836,10 @@
     bo, ig, fg, sg, cg, sqg, exg = pl.pallas_call(
         copy_out,
         out_shape=[shape(v.shape, v.dtype) for v in results],
-        in_specs=[spec] * 7,
+        in_specs=[pl.BlockSpec(memory_space=pl.ANY)] * 7,
         out_specs=[spec] * 7,
-        compiler_params=pltpu.CompilerParams(vmem_limit_bytes=32 * 1024 * 1024),
+        scratch_shapes=[pltpu.SemaphoreType.DMA((7,))],
+        compiler_params=pltpu.CompilerParams(vmem_limit_bytes=62 * 1024 * 1024),
     )(*results)
     return (bo.reshape(inputs.shape), ig.reshape(inputs.shape), fg.T, sg, cg.transpose(1, 0, 2), sqg, exg.T)
 

time: 160 us -> 154 us (0.963)
  local copies, waits for them, and re-layouts: 8.36 us -> 1.27 us
    unnamed x14 -> x0, local copies, waits for them, and re-layouts: 7.1 us -> none
    pallas_call x1, Pallas kernels: 1.91 us -> 3.52 us  [per_device(): pl.pallas_call(copy_out, out_shape=[shape(v.shape, v.dtype) for v in resu...]
where the time goes in v6:
time: 154 us; the launch traced here: 153 us
  Pallas kernels  151 us (98%)
    pallas_call x1, Pallas kernels, per_device(): pl.pallas_call(body, out_shape=[shape((4, PX, CH_DEV), bf16), shape((4, P...  148 us
    pallas_call x1, Pallas kernels, per_device(): pl.pallas_call(copy_out, out_shape=[shape(v.shape, v.dtype) for v in resu...  3.52 us

profile of v6, /device:TPU:2, one launch (start us, length us, event | category | flops | bytes accessed | tf_op | source)
XLA Modules:
  0.0 153.1 jit_solution(2487453192552326413)
XLA Ops:
  0.6 1.3 broadcast_in_dim.15.b4_hbm
  1.9 147.5 %shard_map.180 = (bf16[4,256,66]{2,1,0:T(8,128)(2,1)}, bf16[4,256,66]{2,1,0:T(8,128)(2,1)}, f32[66,2112]{1,0:T(8,128)}, f32[66,2112]{1,0:T(8,128)}, f32[9,66,264...) custom-call(bf16[4,256,66]{2,1,0:T(8,128)(2,1)} %bitcast.15, bf16[4,256,66]{2,1,0:T(8,128)(2,1)} %bitcast.16, ...), custom_call_target="tpu_custom_call" | custom-call | tf_op jit(solution)/shard_map/pallas_call | solution.py:811
  149.4 3.5 %shard_map.181 = (bf16[4,256,66]{2,1,0:T(8,128)(2,1)}, bf16[4,256,66]{2,1,0:T(8,128)(2,1)}, f32[66,2112]{1,0:T(8,128)}, f32[66,2112]{1,0:T(8,128)}, f32[9,66,264...) custom-call(bf16[4,256,66]{2,1,0:T(8,128)(2,1)} %get-tuple-element.21.refs_0_, ...), custom_call_target="tpu_custom_call" | custom-call | tf_op jit(solution)/shard_map/pallas_call | solution.py:836

commit v7 on v6

--- a/solution.py
+++ b/solution.py
@@ -392,15 +392,9 @@
     sq_w = smg[:, :, 0:SQP].reshape(GP, SQP)
     ex_w = smg[:, :, SQP : 2 * SQP].reshape(GP, SQP)
     bh = squeeze_start(split_left(dot, means, sq_w), hb8)
-    for q in range(4):
-        cq[q] = dot_nt(eye, c_in[q]).astype(bf16)
     s2 = group_forward(s2, w2r)
     group_finish(s2)
     spread(w2r, w2g)
-    xb = dot_tn(fbp[0], x_rows) + dot_tn(fbp[1], x_rows)
-    xb_top = xb.astype(bf16)
-    xbt[0:BASIS, :] = xb_top
-    xbt[BASIS:, :] = (xb - xb_top.astype(f32)).astype(bf16)
     squeeze_pre = squeeze_finish(bh, hb8) + sqb[0:1]
     squeeze = squeeze_pre * sigmoid(squeeze_pre)
     excite = sigmoid(split_right(dot_nt, ex_w, squeeze) + bias(2))
@@ -483,6 +477,12 @@
     sls[...] = sl.reshape(4, CB, PX)
     ssl = [copy(sls.at[flip(m, k)], slr.at[k], z, peer(k)) for k in range(1, 4)]
     r1 = reduce_relay(r1, 0)
+    for q in range(4):
+        cq[q] = dot_nt(eye, c_in[q]).astype(bf16)
+    xb = dot_tn(fbp[0], x_rows) + dot_tn(fbp[1], x_rows)
+    xb_top = xb.astype(bf16)
+    xbt[0:BASIS, :] = xb_top
+    xbt[BASIS:, :] = (xb - xb_top.astype(f32)).astype(bf16)
     ssb = group_forward(ssb, sbg)
     group_finish(ssb)
     sb_top = sbg[:, :, 0:BASIS].reshape(GP, BASIS)
@@ -554,20 +554,20 @@
     for k in range(4):
         c2s[k] = coords[:, 640 * k : 640 * (k + 1)].astype(bf16)
     c2g = [copy(c2s.at[flip(m, k)], c2r.at[k], z, peer(k)) for k in range(1, 4)]
+    excite_back = sums_finish(se_, ez)
+    sig_back = excite_back * ex_row * (1.0 - ex_row)
+    be = squeeze_start(split_left(dot, sig_back, ex_w), eb8)
+    for c in c2g:
+        c.wait_recv()
+    c2 = c2s[m].astype(f32) + c2r[1].astype(f32) + c2r[2].astype(f32) + c2r[3].astype(f32)
+    c2z[...] = c2.astype(bf16)
+    c2t = [copy(c2z, c2zr.at[k], flip(z, k), me) for k in range(1, 8)]
     for c in hsw:
         c.wait_recv()
     acc = dot_nt(hbs[m], cols[0])
     for k in range(1, 4):
         acc = acc + dot_nt(hbr[k], cols[k])
     ga[...] = acc
-    excite_back = sums_finish(se_, ez)
-    sig_back = excite_back * ex_row * (1.0 - ex_row)
-    be = squeeze_start(split_left(dot, sig_back, ex_w), eb8)
-    for c in c2g:
-        c.wait_recv()
-    c2 = c2s[m].astype(f32) + c2r[1].astype(f32) + c2r[2].astype(f32) + c2r[3].astype(f32)
-    c2z[...] = c2.astype(bf16)
-    c2t = [copy(c2z, c2zr.at[k], flip(z, k), me) for k in range(1, 8)]
     halo_finish(exta, halo_a)
     squeeze_back = squeeze_finish(be, eb8) * slope(squeeze_pre)
     means_back = split_right(dot_nt, sq_w, squeeze_back)

time: 154 us -> 155 us (level)
  no operation moved by 1% of the time
where the time goes in v7:
time: 155 us; the launch traced here: 154 us
  Pallas kernels  152 us (98%)
    pallas_call x1, Pallas kernels, per_device(): pl.pallas_call(body, out_shape=[shape((4, PX, CH_DEV), bf16), shape((4, P...  148 us
    pallas_call x1, Pallas kernels, per_device(): pl.pallas_call(copy_out, out_shape=[shape(v.shape, v.dtype) for v in resu...  3.52 us

profile of v7, /device:TPU:2, one launch (start us, length us, event | category | flops | bytes accessed | tf_op | source)
XLA Modules:
  0.0 153.8 jit_solution(6458815019669194005)
XLA Ops:
  0.6 1.3 broadcast_in_dim.15.b4_hbm
  1.9 148.2 %shard_map.180 = (bf16[4,256,66]{2,1,0:T(8,128)(2,1)}, bf16[4,256,66]{2,1,0:T(8,128)(2,1)}, f32[66,2112]{1,0:T(8,128)}, f32[66,2112]{1,0:T(8,128)}, f32[9,66,264...) custom-call(bf16[4,256,66]{2,1,0:T(8,128)(2,1)} %bitcast.15, bf16[4,256,66]{2,1,0:T(8,128)(2,1)} %bitcast.16, ...), custom_call_target="tpu_custom_call" | custom-call | tf_op jit(solution)/shard_map/pallas_call | solution.py:811
  150.1 3.5 %shard_map.181 = (bf16[4,256,66]{2,1,0:T(8,128)(2,1)}, bf16[4,256,66]{2,1,0:T(8,128)(2,1)}, f32[66,2112]{1,0:T(8,128)}, f32[66,2112]{1,0:T(8,128)}, f32[9,66,264...) custom-call(bf16[4,256,66]{2,1,0:T(8,128)(2,1)} %get-tuple-element.21.refs_0_, ...), custom_call_target="tpu_custom_call" | custom-call | tf_op jit(solution)/shard_map/pallas_call | solution.py:836
